TPU v7x, 512 devices: a whole 4x4x16 slice. The times are simulated.
512 devices in a mesh: ctx: 32 (over y, x, core), ep: 16 (over z).
Axes of the slice: x: 4, y: 4, z: 16, core: 2. Of those that a mesh axis runs over, the one named last changes fastest.
Arguments:
- queries: bfloat16 [64, 64, 576], P('ep'), may hold values from -18 to 18
- latent_cache: bfloat16 [64, 3072, 576], P('ep', 'ctx'), may hold values from -4.5 to 4.5
- lengths: int32 [64], P('ep'), may hold values from 2 to 3072, as said below
- w_uv: bfloat16 [64, 512, 128], P('ctx'), may hold values from -4 to 4
- w_out: bfloat16 [8192, 3584], P('ctx'), may hold values from -0.0625 to 0.0625
- residual: bfloat16 [64, 3584], P('ep', 'ctx'), may hold values from -4 to 4
- norm_gain: float32 [3584], P('ctx'), may hold values from 0.5 to 1.5
- router: bfloat16 [16, 3584], P('ep', 'ctx'), may hold values from -0.09375 to 0.09375
- w_gate: bfloat16 [16, 3584, 2048], P('ep', 'ctx'), may hold values from -0.09375 to 0.09375
- w_up: bfloat16 [16, 3584, 2048], P('ep', 'ctx'), may hold values from -0.09375 to 0.09375
- w_down: bfloat16 [16, 2048, 3584], P('ep', None, 'ctx'), may hold values from -0.125 to 0.125
- expert_ids: int32 [64, 8], P('ep'), may hold values from 0 to 15, all different within a row; in each aligned block of 4 rows (0 to 3, 4 to 7, ...) at most 4 rows name the same one
Outputs:
- mixed: float32 [64, 3584], P('ep', 'ctx')
Inputs may be any that keep to these rules, and one draw needn't show every extreme that they name: `expert_ids`: each row names 8 different experts; the 4 rows of one ep index name one expert at most 4 times, and exactly 4 times for some expert. `lengths`: every row reads at least its first two positions; some row reads all 3072.
All inputs are finite; a program needn't handle non-finite values.
Results may differ from a plain program's by a relative error of at most 0.019.
Values may be sent and summed in bfloat16 or wider, within the bound.
A program may use at most 64 MiB of HBM per device.

v0:
```python
import jax
import jax.numpy as jnp
from jax import lax
from jax.sharding import PartitionSpec as P

D = 3584
LATENT = 512


score_scale = 192.0 ** (-0.5)
floor_value = -1e30
norm_eps = 1e-06
route_scale = 2.5


def merged_2(x, axis, combine):
    everything = jax.tree.map(lambda part: lax.all_gather(part, axis), x)
    initial = jax.tree.map(lambda part: part[0], everything)

    def hop(k, so_far):
        return combine(so_far, jax.tree.map(lambda part: part[k], everything))

    return lax.fori_loop(1, lax.axis_size(axis), hop, initial)


def combine(first, second):
    peak = jnp.maximum(first[0], second[0])
    left = jnp.exp(first[0] - peak)
    right = jnp.exp(second[0] - peak)
    return (
        peak,
        left * first[1] + right * second[1],
        left[..., None] * first[2] + right[..., None] * second[2],
    )


def per_device(
    queries,
    latent_cache,
    lengths,
    w_uv,
    w_out,
    residual,
    norm_gain,
    router,
    w_gate,
    w_up,
    w_down,
    expert_ids,
):
    row_count = queries.shape[0]
    span = latent_cache.shape[1]
    positions = lax.axis_index("ctx") * span + jnp.arange(span)
    valid = (positions[None, :] < lengths[:, None])[:, None, :]
    scores = (
        jnp.einsum("rhk,rsk->rhs", queries, latent_cache, preferred_element_type=jnp.float32)
        * score_scale
    )
    masked = jnp.where(valid, scores, floor_value)
    local_peak = jnp.max(masked, axis=2)
    weights = jnp.where(valid, jnp.exp(masked - local_peak[..., None]), 0.0).astype(jnp.bfloat16)
    totals = jnp.sum(weights.astype(jnp.float32), axis=2)
    partial_sum = jnp.einsum(
        "rhs,rsl->rhl", weights, latent_cache[:, :, :LATENT], preferred_element_type=jnp.float32
    )
    head_count = w_uv.shape[0]
    merged = merged_2((local_peak, totals, partial_sum), "ctx", combine)
    first_head = lax.axis_index("ctx") * head_count
    shares = lax.dynamic_slice_in_dim(merged[2], first_head, head_count, 1)
    denoms = lax.dynamic_slice_in_dim(merged[1], first_head, head_count, 1)
    latent_out = (shares / denoms[..., None]).astype(jnp.bfloat16)
    value_rows = jnp.einsum("rhl,hlv->rhv", latent_out, w_uv, preferred_element_type=jnp.float32)
    value_rows = value_rows.astype(jnp.bfloat16).reshape(row_count, -1)
    attended = lax.psum_scatter(
        lax.dot_general(
            w_out, value_rows, (((0,), (1,)), ((), ())), preferred_element_type=jnp.float32
        ),
        "ctx",
        scatter_dimension=0,
        tiled=True,
    )
    stream = residual.astype(jnp.float32) + attended.T
    hidden = stream.astype(jnp.bfloat16)
    top_count = expert_ids.shape[1]
    expert_total = lax.axis_size("ep")
    capacity = 2 * row_count * top_count // expert_total
    flat_ids = expert_ids.reshape(-1)
    table = (flat_ids[:, None] == jnp.arange(expert_total)[None, :]).astype(jnp.int32)
    earlier = jnp.cumsum(table, axis=0) - table
    slot_rank = jnp.sum(table * earlier, axis=1)
    target = flat_ids * capacity + slot_rank
    placing = (target[:, None] == jnp.arange(expert_total * capacity)[None, :]).astype(jnp.bfloat16)
    routing = jnp.sum(placing.reshape(row_count, top_count, -1), axis=1)
    outgoing = lax.dot_general(
        routing, hidden, (((0,), (0,)), ((), ())), preferred_element_type=jnp.float32
    )
    width_local = hidden.shape[1]
    outgoing = outgoing.astype(jnp.bfloat16).reshape(expert_total, capacity, width_local)
    received = lax.all_to_all(outgoing, "ep", split_axis=0, concat_axis=0, tiled=True)
    tokens = received.reshape(-1, width_local)
    wide_tokens = tokens.astype(jnp.float32)
    scaled = (wide_tokens * norm_gain).astype(jnp.bfloat16)
    squares = jnp.sum(wide_tokens * wide_tokens, axis=1)
    gate_part = jnp.dot(scaled, w_gate[0], preferred_element_type=jnp.float32)
    up_part = jnp.dot(scaled, w_up[0], preferred_element_type=jnp.float32)
    logit_part = jnp.dot(scaled, router[0], preferred_element_type=jnp.float32)
    gate_full, up_full, square_sum, logits = lax.psum(
        (gate_part, up_part, squares, logit_part), "ctx"
    )
    inverse = lax.rsqrt(square_sum / D + norm_eps)
    activated = (jax.nn.silu(gate_full * inverse[:, None]) * (up_full * inverse[:, None])).astype(
        jnp.bfloat16
    )
    gating = jax.nn.sigmoid(logits * inverse).astype(jnp.bfloat16)
    expert_out = jnp.dot(activated, w_down[0], preferred_element_type=jnp.float32)
    weighted = (expert_out * gating.astype(jnp.float32)[:, None]).astype(jnp.bfloat16)
    returned, gates_back = (
        lax.all_to_all(
            weighted.reshape(expert_total, capacity, width_local),
            "ep",
            split_axis=0,
            concat_axis=0,
            tiled=True,
        ),
        lax.all_to_all(
            gating.reshape(expert_total, capacity), "ep", split_axis=0, concat_axis=0, tiled=True
        ),
    )
    numer = jnp.dot(routing, returned.reshape(-1, width_local), preferred_element_type=jnp.float32)
    denom = jnp.dot(routing, gates_back.reshape(-1), preferred_element_type=jnp.float32)
    mixed = stream + route_scale * numer / denom[:, None]
    return mixed


def solution(mesh):
    in_specs = (
        P("ep", None, None),
        P("ep", "ctx", None),
        P("ep"),
        P("ctx", None, None),
        P("ctx", None),
        P("ep", "ctx"),
        P("ctx"),
        P("ep", "ctx"),
        P("ep", "ctx", None),
        P("ep", "ctx", None),
        P("ep", None, "ctx"),
        P("ep", None),
    )
    out_specs = P("ep", "ctx")
    return jax.shard_map(
        per_device, mesh=mesh, in_specs=in_specs, out_specs=out_specs, check_vma=False
    )
```

profile of v0, /device:TPU:1, one launch (start us, length us, event | category | flops | bytes accessed | tf_op | source)
XLA Modules:
  0.0 434.4 jit_solution(11625885174541378309)
XLA Ops:
  7.4 1.5 fusion.30
  8.9 2.1 fusion.13
  11.8 27.9 %all-gather.4 = f32[32,4,64]{2,1,0:T(4,128)S(1)} all-gather(f32[1,4,64]{2,1,0:T(4,128)S(1)} %bitcast.82), channel_id=3, replica_groups=mesh['ctx'=32,'ep'=16] {'ctx'}, dimensions={0}, use_global_device_ids=true | all-gather | bytes 33792 | tf_op jit(solution)/shard_map/all_gather | solution.py:17
  39.7 24.2 %all-gather.3 = f32[32,4,64]{2,1,0:T(4,128)S(1)} all-gather(f32[1,4,64]{2,1,0:T(4,128)S(1)} %bitcast.80), channel_id=2, replica_groups=mesh['ctx'=32,'ep'=16] {'ctx'}, dimensions={0}, use_global_device_ids=true | all-gather | bytes 33792 | tf_op jit(solution)/shard_map/all_gather | solution.py:17
  63.9 40.8 %all-gather.7.cloned.1.call-done = f32[128,64,512]{2,1,0:T(8,128)} async-done(((f32[4,64,512]{2,1,0:T(8,128)}), f32[128,64,512]{2,1,0:T(8,128)}) %all-gather.7.cloned.1.call-update) | async-done | bytes 16777232 | tf_op jit(solution)/shard_map/all_gather | solution.py:17
  105.8 39.3 %while.19 = (s32[]{:T(128)}, f32[4,64]{1,0:T(4,128)S(1)}, f32[4,64]{1,0:T(4,128)S(1)}, f32[4,64,512]{2,1,0:T(8,128)S(1)}, f32[32,4,64]{2,1,0:T(4,128)S(1)}, /*in...) while((s32[]{:T(128)}, f32[4,64]{1,0:T(4,128)S(1)}, ...), condition=%wide.region_3.4_spmd, body=%wide.region_2.3_spmd.sunk | while | flops 394757 | bytes 1583255 | solution.py:23
  105.9 1.2 fusion.46
  107.2 1.2 fusion.46
  108.5 1.2 fusion.46
  112.2 1.2 fusion.46
  113.5 1.2 fusion.46
  114.8 1.2 fusion.46
  116.0 1.2 fusion.46
  121.1 1.2 fusion.46
  122.4 1.2 fusion.46
  123.6 1.2 fusion.46
  124.9 1.2 fusion.46
  128.7 1.2 fusion.46
  130.0 1.2 fusion.46
  131.2 1.2 fusion.46
  132.5 1.2 fusion.46
  136.3 1.2 fusion.46
  137.6 1.2 fusion.46
  145.8 1.8 copy.19
  147.8 99.2 %reduce-scatter.4.cloned.1.call-done = f32[112,4]{1,0:T(8,128)} async-done(((f32[3584,4]{1,0:T(8,128)}), f32[112,4]{1,0:T(8,128)}) %reduce-scatter.4.cloned.1.call-update) | async-done | bytes 1808
  248.1 23.2 %all_to_all.20 = bf16[16,4,112]{2,1,0:T(4,128)(2,1)S(1)} all-to-all(bf16[16,4,112]{2,1,0:T(4,128)(2,1)S(1)} %bitcast.79), channel_id=1, replica_groups=mesh['ctx'=32,'ep'=16] {'ep'}, dimensions={0} | all-to-all | bytes 28672 | tf_op jit(solution)/shard_map/all_to_all | solution.py:99
  273.7 65.8 %all-reduce = (f32[64]{0:T(128)S(1)}, f32[64]{0:T(128)S(1)}) all-reduce(f32[64]{0:T(128)S(1)} %reduce_sum.48, f32[64]{0:T(128)S(1)} %convolution_bitcast_fusion.1), channel_id=1, replica_groups=mesh['ctx'=32,'ep'=16] {'ctx'}, use_global_device_ids=true, to_apply=%region_10.11 | all-reduce | flops 128 | bytes 1024 | tf_op jit(solution)/shard_map/psum | solution.py:107
  339.6 13.8 %all_to_all.21 = bf16[16,1,4]{2,1,0:T(2,128)(2,1)S(1)} all-to-all(bf16[16,1,4]{2,1,0:T(2,128)(2,1)S(1)} %all_to_all.16), channel_id=1, replica_groups=mesh['ctx'=32,'ep'=16] {'ep'}, dimensions={0} | all-to-all | bytes 256 | tf_op jit(solution)/shard_map/all_to_all | solution.py:125
  353.5 48.1 %all-reduce.4.cloned.1.call-done = (f32[64,2048]{1,0:T(8,128)}, f32[64,2048]{1,0:T(8,128)}) async-done(((f32[64,2048]{1,0:T(8,128)}, f32[64,2048]{1,0:T(8,128)}), (f32[64,2048]{1,0:T(8,128)}, f32[64,2048]{1,0:T(8,128)})) %all-reduce.4.cloned.1.call-update) | async-done | bytes 1048592 | tf_op jit(solution)/shard_map/psum | solution.py:107
  401.6 2.2 fusion.4
  403.7 12.0 %all-to-all-start.1 = ((bf16[16,4,112]{2,1,0:T(4,128)(2,1)}), bf16[16,4,112]{2,1,0:T(4,128)(2,1)S(1)}, u32[]{:S(2)}, u32[]{:S(2)}) async-start(bf16[16,4,112]{2,1,0:T(4,128)(2,1)} %bitcast.20), calls=%async_computation.1 | async-start | bytes 32768 | tf_op jit(solution)/shard_map/all_to_all | solution.py:118
  415.9 11.3 %all-to-all-done.1 = bf16[16,4,112]{2,1,0:T(4,128)(2,1)S(1)} async-done(((bf16[16,4,112]{2,1,0:T(4,128)(2,1)}), bf16[16,4,112]{2,1,0:T(4,128)(2,1)S(1)}, u32[]{:S(2)}, u32[]{:S(2)}) %all-to-all-start.1) | async-done | bytes 14368 | tf_op jit(solution)/shard_map/all_to_all | solution.py:118
  (98 shorter events, 25.8 us)
Async XLA Ops:
  6.5 138.7 %copy-start = (bf16[256,3584]{1,0:T(8,128)(2,1)S(1)}, bf16[256,3584]{1,0:T(8,128)(2,1)}, u32[]{:S(2)}) copy-start(bf16[256,3584]{1,0:T(8,128)(2,1)} %param.18) | copy-start | bytes 5505028
  6.5 4.6 %copy-start.4 = (s32[4,8]{1,0:T(4,128)S(1)}, s32[4,8]{1,0:T(4,128)}, u32[]{:S(2)}) copy-start(s32[4,8]{1,0:T(4,128)} %param.25) | copy-start | bytes 388
  6.5 98.2 %all-gather.7.cloned.1.call-start = ((), (), s32[]{:S(2)}) async-start(), calls=%async_computation.4 | async-start | bytes 17301504 | tf_op jit(solution)/shard_map/all_gather | solution.py:17
  11.0 235.9 %reduce-scatter.4.cloned.1.call-start = ((), (), s32[]{:S(2)}) async-start(), calls=%async_computation.5 | async-start | bytes 1892352
  105.8 39.4 %copy-start.3 = (bf16[2,512,128]{2,1,0:T(8,128)(2,1)S(1)}, bf16[2,512,128]{2,1,0:T(8,128)(2,1)}, u32[]{:S(2)}) copy-start(bf16[2,512,128]{2,1,0:T(8,128)(2,1)} %param.17) | copy-start | bytes 786436
  145.8 102.1 %copy-start.5 = (bf16[4,112]{1,0:T(4,128)(2,1)S(1)}, bf16[4,112]{1,0:T(4,128)(2,1)}, u32[]{:S(2)}) copy-start(bf16[4,112]{1,0:T(4,128)(2,1)} %param.19) | copy-start | bytes 2692
  145.8 125.5 %copy-start.6 = (f32[112]{0:T(128)S(1)}, f32[112]{0:T(128)}, u32[]{:S(2)}) copy-start(f32[112]{0:T(128)} %param.20) | copy-start | bytes 1348
  145.8 125.6 %copy-start.1 = (bf16[1,112,2048]{2,1,0:T(8,128)(2,1)S(1)}, bf16[1,112,2048]{2,1,0:T(8,128)(2,1)}, u32[]{:S(2)}) copy-start(bf16[1,112,2048]{2,1,0:T(8,128)(2,1)} %param.22) | copy-start | bytes 1376260
  147.6 124.8 %copy-start.2 = (bf16[1,112,2048]{2,1,0:T(8,128)(2,1)S(1)}, bf16[1,112,2048]{2,1,0:T(8,128)(2,1)}, u32[]{:S(2)}) copy-start(bf16[1,112,2048]{2,1,0:T(8,128)(2,1)} %param.23) | copy-start | bytes 1376260
  147.6 125.9 %copy-start.8 = (bf16[1,112]{1,0:T(2,128)(2,1)S(1)}, bf16[1,112]{1,0:T(2,128)(2,1)}, u32[]{:S(2)}) copy-start(bf16[1,112]{1,0:T(2,128)(2,1)} %param.21) | copy-start | bytes 676
  147.6 253.9 %copy-start.7 = (bf16[1,2048,112]{1,2,0:T(8,128)(2,1)S(1)}, bf16[1,2048,112]{1,2,0:T(8,128)(2,1)}, u32[]{:S(2)}) copy-start(bf16[1,2048,112]{1,2,0:T(8,128)(2,1)} %param.24) | copy-start | bytes 1376260
  147.6 253.9 %all-reduce.4.cloned.1.call-start = ((), (), s32[]{:S(2)}) async-start(), calls=%async_computation.6 | async-start | bytes 2097152 | tf_op jit(solution)/shard_map/psum | solution.py:107
  403.7 23.4 %all-to-all-start.1 = ((bf16[16,4,112]{2,1,0:T(4,128)(2,1)}), bf16[16,4,112]{2,1,0:T(4,128)(2,1)S(1)}, u32[]{:S(2)}, u32[]{:S(2)}) async-start(bf16[16,4,112]{2,1,0:T(4,128)(2,1)} %bitcast.20), calls=%async_computation.1 | async-start | bytes 32768 | tf_op jit(solution)/shard_map/all_to_all | solution.py:118
Sparse Core Ops, SparseCore 0:
  11.2 93.5 all-gather.6
  147.7 99.1 reduce-scatter.3
  273.6 127.9 all-reduce.3
where the time goes:
time: 438 us; the launch traced here: 434 us
  waiting for transfers between devices  199 us (45%)
  blocking collectives  155 us (35%)
  other arithmetic  40.1 us (9%)
  between operations  13.3 us (3%)
  starting transfers between devices  12.1 us (3%)
  matrix products  9.44 us (2%)
    unnamed x4, waiting for transfers between devices  99.2 us
    psum x1, blocking collectives, per_device(): lax.psum((gate_part, up_part, squares, logit_part), 'ctx')  65.8 us
    all_gather x2, blocking collectives, merged_2(): everything = jax.tree.map(lambda part: lax.all_gather(part, axis), x)  52.1 us
    psum x1, waiting for transfers between devices, per_device(): lax.psum((gate_part, up_part, squares, logit_part), 'ctx')  48.1 us
    all_gather x1, waiting for transfers between devices, merged_2(): everything = jax.tree.map(lambda part: lax.all_gather(part, axis), x)  40.8 us
    add x31, other arithmetic, combine(): left[..., None] * first[2] + right[..., None] * second[2]  37.6 us
    all_to_all x1, blocking collectives, per_device(): lax.all_to_all(outgoing, 'ep', split_axis=0, concat_axis=0, tiled=True)  23.2 us
    all_to_all x1, blocking collectives, per_device(): lax.all_to_all(gating.reshape(expert_total, capacity), 'ep', split_axis=0...  13.8 us
  transfers between devices with their start and end apart: 4, of which 4 were waited for; matrix products, arithmetic and copies ran while one was open for 0% of the time, Pallas kernels for 0%

commit v1 on v0

v1 whole, which is shorter than its diff:
```python
import functools

import jax
import jax.numpy as jnp
from jax import lax
from jax.experimental import pallas as pl
from jax.experimental.pallas import tpu as pltpu
from jax.sharding import PartitionSpec as P

SCALE = 192.0 ** (-0.5)
FLOOR = -1e30
EPS = 1e-06
ROUTE = 2.5
LATENT = 512
WIDE = 128
MESH = pl.DeviceIdType.MESH
BF16, F32, I32 = jnp.bfloat16, jnp.float32, jnp.int32


def iota(shape, dim):
    return lax.broadcasted_iota(I32, shape, dim)


def split_two(x):
    high = x.astype(BF16).astype(F32)
    return high, x - high


def kernel(
    nc,
    ne,
    q_h, cache_h, len_h, wuv_h, wout_h, res_h, gain_h, router_h, wg_h, wu_h, wd_h, ids_h,
    out_ref,
    q_v, cache_v, len_s, wuv_v, wout_v, res_v, gain_v, router_v, wg_v, wu_v, wd_v, ids_v,
    pack, hit_v, st_v, hid_v,
    s1, r1, s2, r2, r3, s4, r4, s5, r5, s6, r6,
    load_sem, pair_send, pair_recv, ssem, rsem,
):
    nk, half = nc // 2, ne // 2
    width = res_h.shape[1]
    span = cache_h.shape[1]
    rows = 8 * nc
    batch = 4 * half
    c, e = lax.axis_index("ctx"), lax.axis_index("ep")
    k, core = c // 2, lax.rem(c, 2)
    side = e // half
    owner = core == side
    partner = 2 * k + 1 - core

    def load(n, src, dst):
        return pltpu.make_async_copy(src, dst, load_sem.at[n])

    loads = [
        load(0, q_h, q_v),
        load(1, cache_h, cache_v),
        load(2, len_h, len_s),
        load(3, res_h, res_v),
        load(4, gain_h, gain_v),
        load(5, router_h, router_v),
        load(6, ids_h, ids_v),
        load(7, wuv_h, wuv_v),
        load(8, wout_h, wout_v),
        load(9, wg_h.at[0], wg_v.at[core, pl.ds(0, width)]),
        load(10, wu_h.at[0], wu_v.at[core, pl.ds(0, width)]),
        load(11, wd_h.at[0], wd_v.at[core]),
    ]
    for one in loads:
        one.start()

    barrier = pltpu.get_barrier_semaphore()

    def greet_ctx(i, _):
        pl.semaphore_signal(barrier, inc=1, device_id=(lax.rem(c + i, nc), e), device_id_type=MESH)
        return 0

    def greet_ep(i, _):
        for f in range(2):
            pl.semaphore_signal(
                barrier, inc=1, device_id=(2 * k + f, lax.rem(e + i, ne)), device_id_type=MESH
            )
        return 0

    lax.fori_loop(1, nc, greet_ctx, 0)
    lax.fori_loop(1, ne, greet_ep, 0)

    def remote(src, dst, send, recv, to):
        return pltpu.make_async_remote_copy(
            src_ref=src, dst_ref=dst, send_sem=send, recv_sem=recv, device_id=to, device_id_type=MESH
        )

    def drain(ref, sem):
        pltpu.make_async_copy(ref, ref, sem).wait()

    for one in loads[2:7]:
        one.wait()
    pack[pl.ds(core, 1)] = jnp.zeros((1, 16, WIDE), F32)
    wide_res = res_v[...].astype(F32)
    pack[core, 0:8, 0:width] = jnp.concatenate([wide_res, wide_res], axis=0)
    pack[core, 8:9, 0:width] = gain_v[...]
    pack[core, 9:10, 0:width] = router_v[...].astype(F32)
    blank = jnp.zeros((2, WIDE - width, wg_v.shape[2]), BF16)
    wg_v[:, width:WIDE, :] = blank
    wu_v[:, width:WIDE, :] = blank
    ids8 = jnp.concatenate([ids_v[...], ids_v[...]], axis=0)
    for x in range(ne):
        hit = jnp.max(jnp.where(ids8 == x, 1.0, 0.0), axis=1, keepdims=True)
        hit_v[x] = jnp.broadcast_to(hit, (8, WIDE))

    loads[0].wait()
    row = iota((rows, rows), 0)
    want = (row & 3) * (2 * nc) + 2 * (row >> 3) + ((row >> 2) & 1)
    order = jnp.where(iota((rows, rows), 1) == want, 1.0, 0.0).astype(BF16)
    q = q_v[...].reshape(rows, q_v.shape[2])
    q = jnp.dot(order, q, preferred_element_type=F32).astype(BF16)
    loads[1].wait()
    keys = cache_v[...].reshape(4 * span, cache_v.shape[2])
    scores = lax.dot_general(q, keys, (((1,), (1,)), ((), ())), preferred_element_type=F32) * SCALE
    col = iota((1, 4 * span), 1)
    col_row = jnp.zeros_like(col)
    limit = jnp.full_like(col, len_s[0])
    for r in range(1, 4):
        past = col >= r * span
        col_row = jnp.where(past, r, col_row)
        limit = jnp.where(past, len_s[r], limit)
    position = c * span + col - col_row * span
    col_row = jnp.where(position < limit, col_row, -1)
    valid = (iota((rows, 4 * span), 0) & 3) == col_row
    masked = jnp.where(valid, scores, FLOOR)
    peak = jnp.max(masked, axis=1, keepdims=True).astype(BF16).astype(F32)
    weights = jnp.where(valid, jnp.exp(masked - peak), 0.0).astype(BF16)
    total = jnp.sum(weights.astype(F32), axis=1, keepdims=True)
    summed = jnp.dot(weights, keys[:, :LATENT], preferred_element_type=F32)
    summed = summed.reshape(nc, 8, LATENT)
    hl = LATENT // 2
    s1[:, :, 0:hl] = jnp.concatenate([summed[:, :, 0:hl], summed[:, :, hl:]], axis=1).astype(BF16)
    high, low = split_two(total)
    peaks = jnp.broadcast_to(peak, (rows, WIDE)).reshape(nc, 8, WIDE)
    totals = jnp.where(iota((rows, WIDE), 1) < 64, high, low).reshape(nc, 8, WIDE)
    s1[:, :, hl:] = jnp.concatenate([peaks, totals], axis=1).astype(BF16)
    r1[pl.ds(c, 1)] = s1[pl.ds(c, 1)]

    pl.semaphore_wait(barrier, nc - 1 + 2 * (ne - 1))

    def send_1(i, _):
        d = lax.rem(c + i, nc)
        remote(s1.at[d], r1.at[c], ssem.at[0], rsem.at[0], (d, e)).start()
        return 0

    lax.fori_loop(1, nc, send_1, 0)

    mine = pl.ds(0, width)
    swaps = [
        remote(pack.at[core], pack.at[core], pair_send.at[0], pair_recv.at[0], (partner, e)),
        remote(wg_h.at[0], wg_v.at[core, mine], pair_send.at[1], pair_recv.at[1], (partner, e)),
        remote(wu_h.at[0], wu_v.at[core, mine], pair_send.at[2], pair_recv.at[2], (partner, e)),
        remote(wd_h.at[0], wd_v.at[core], pair_send.at[3], pair_recv.at[3], (partner, e)),
    ]
    for one in swaps:
        one.start()

    drain(r1.at[pl.ds(0, nc - 1)], rsem.at[0])
    stats = r1[:, :, hl:].astype(F32)
    peaks = stats[:, 0:8]
    factor = jnp.exp(peaks - jnp.max(peaks, axis=0)[None])
    denom = jnp.sum(factor * stats[:, 8:16], axis=0)
    denom = denom[:, 0:1] + denom[:, 64:65]
    columns = []
    for top in range(2):
        for a in range(0, hl, WIDE):
            block = r1[:, :, a : a + WIDE].astype(F32)[:, 8 * top : 8 * top + 8]
            columns.append(jnp.sum(factor * block, axis=0))
    latent = (jnp.concatenate(columns, axis=1) / denom).astype(BF16)

    loads[7].wait()
    first = jnp.dot(latent, wuv_v[0], preferred_element_type=F32)
    second = jnp.dot(latent, wuv_v[1], preferred_element_type=F32)
    upper = iota((8, WIDE), 0) < 4
    lane = iota((8, WIDE), 1)
    values = jnp.concatenate(
        [
            jnp.where(upper, first, pltpu.roll(first, 4, 0)),
            jnp.where(upper, pltpu.roll(second, 4, 0), second),
        ],
        axis=1,
    ).astype(BF16)
    loads[8].wait()
    group = min(4, nk)
    for g in range(0, nk, group):
        begin, size = 2 * width * g, 2 * width * group
        part = jnp.dot(values, wout_v[:, begin : begin + size], preferred_element_type=F32)
        part = jnp.concatenate([part, jnp.zeros((8, WIDE), F32)], axis=1)
        for i in range(group):
            a = 2 * width * i
            s2[g + i] = jnp.where(upper, part[:, a : a + WIDE], part[:, a + width : a + width + WIDE])

    def send_2(i, _):
        d = lax.rem(k + i, nk)
        remote(s2.at[d], r2.at[c], ssem.at[1], rsem.at[1], (2 * d + side, e)).start()
        return 0

    @pl.when(owner)
    def _():
        r2[pl.ds(c, 1)] = s2[pl.ds(k, 1)]

    @pl.when(jnp.logical_not(owner))
    def _():
        send_2(0, 0)

    lax.fori_loop(1, nk, send_2, 0)

    swaps[0].wait_recv()

    @pl.when(owner)
    def _():
        drain(r2.at[pl.ds(0, nc - 1)], rsem.at[1])
        stream = jnp.sum(r2[...], axis=0) + jnp.where(upper, pack[0, 0:8], pack[1, 0:8])
        stream = jnp.where(lane < width, stream, 0.0)
        hidden = stream.astype(BF16).astype(F32)
        hid_v[...] = hidden
        st_v[...] = stream
        r3[pl.ds(lax.rem(e, half), 1)] = hidden[None]

        def send_3(i, _):
            z = lax.rem(e + i, ne)
            remote(hid_v, r3.at[lax.rem(e, half)], ssem.at[2], rsem.at[2], (c, z)).start()
            return 0

        lax.fori_loop(1, ne, send_3, 0)
        remote(st_v, st_v, pair_send.at[4], pair_recv.at[4], (partner, e)).start()
        drain(r3.at[pl.ds(0, half - 1)], rsem.at[2])

    @pl.when(jnp.logical_not(owner))
    def _():
        drain(r3, rsem.at[2])

    got = r3[...]
    turned = pltpu.roll(got, 4, 1)
    top3 = iota((half // 2, 8, WIDE), 1) < 4
    got, turned = got.reshape(half // 2, 2, 8, WIDE), turned.reshape(half // 2, 2, 8, WIDE)
    tokens = [
        jnp.where(top3, got[:, 0], turned[:, 1]).reshape(batch, WIDE),
        jnp.where(top3, turned[:, 0], got[:, 1]).reshape(batch, WIDE),
    ]
    squares = jnp.sum(tokens[0] * tokens[0] + tokens[1] * tokens[1], axis=1, keepdims=True)
    scaled = [(tokens[f] * pack[f, 8:9, :]).astype(BF16) for f in range(2)]
    logits = jnp.sum(
        scaled[0].astype(F32) * pack[0, 9:10, :] + scaled[1].astype(F32) * pack[1, 9:10, :],
        axis=1,
        keepdims=True,
    )
    scaled = jnp.concatenate(scaled, axis=1)

    lane16 = iota((16, WIDE), 1)
    block = jnp.zeros((16, WIDE), F32)
    place = 0
    for stat in (squares, logits):
        for piece in split_two(stat):
            for a in range(0, batch, 16):
                block = jnp.where(lane16 == place, piece[a : a + 16], block)
                place += 1
    block = block.astype(BF16)
    for n in (9, 10):
        loads[n].wait()
        swaps[n - 8].wait_recv()
    gate = jnp.dot(scaled, wg_v[...].reshape(2 * WIDE, -1), preferred_element_type=F32).astype(BF16)
    up = jnp.dot(scaled, wu_v[...].reshape(2 * WIDE, -1), preferred_element_type=F32).astype(BF16)
    for d in range(nk):
        s4[d, 0:batch] = gate[:, d * WIDE : (d + 1) * WIDE]
        s4[d, batch : 2 * batch] = up[:, d * WIDE : (d + 1) * WIDE]
        s4[d, 2 * batch :] = block
    r4[pl.ds(k, 1)] = s4[pl.ds(k, 1)]

    def send_4(i, _):
        d = lax.rem(k + i, nk)
        remote(s4.at[d], r4.at[k], ssem.at[3], rsem.at[3], (2 * d + core, e)).start()
        return 0

    lax.fori_loop(1, nk, send_4, 0)
    drain(r4.at[pl.ds(0, nk - 1)], rsem.at[3])
    sums = jnp.sum(r4[...].astype(F32), axis=0)
    gate, up, block = sums[0:batch], sums[batch : 2 * batch], sums[2 * batch :]
    parts = batch // 16

    def column(n):
        pair = block[:, n * parts : (n + 1) * parts] + block[:, (n + 1) * parts : (n + 2) * parts]
        return jnp.concatenate([pair[:, a : a + 1] for a in range(parts)], axis=0)

    inverse = lax.rsqrt(column(0) / (width * nc) + EPS)
    score = jax.nn.sigmoid(column(2) * inverse).astype(BF16).astype(F32)
    gate = gate * inverse
    act = gate / (1.0 + jnp.exp(-gate)) * (up * inverse) * score
    act = act.astype(BF16)

    s5[...] = act
    r5[pl.ds(k, 1)] = act[None]

    def send_5(i, _):
        d = lax.rem(k + i, nk)
        remote(s5, r5.at[k], ssem.at[4], rsem.at[4], (2 * d + core, e)).start()
        return 0

    lax.fori_loop(1, nk, send_5, 0)
    loads[11].wait()
    swaps[3].wait_recv()
    drain(r5.at[pl.ds(0, nk - 1)], rsem.at[4])
    act = jnp.concatenate([r5[d] for d in range(nk)], axis=1)
    shown = jnp.broadcast_to(score, (batch, WIDE - width))
    for f in range(2):
        made = jnp.dot(act, wd_v[f], preferred_element_type=F32)
        made = jnp.concatenate([made, shown], axis=1)
        s6[f] = made.reshape(half // 2, 8, WIDE)

    def send_6(i, _):
        t = lax.rem(e + i, half)
        z = half * core + t
        for f in range(2):
            @pl.when(jnp.logical_not((f == core) & (z == e)))
            def _():
                remote(s6.at[f, t // 2], r6.at[e], ssem.at[5], rsem.at[5], (2 * k + f, z)).start()
        return 0

    lax.fori_loop(0, half, send_6, 0)

    @pl.when(owner)
    def _():
        r6[pl.ds(e, 1)] = s6[core, pl.ds(lax.rem(e, half) // 2, 1)]
        drain(r6.at[pl.ds(0, ne - 1)], rsem.at[5])

    @pl.when(jnp.logical_not(owner))
    def _():
        drain(r6, rsem.at[5])
        pltpu.make_async_copy(st_v, st_v, pair_recv.at[4]).wait()

    mixed = jnp.sum(jnp.where(hit_v[...] > 0.0, r6[...], 0.0), axis=0)
    mixed = jnp.where(lax.rem(e, 2) == 1, pltpu.roll(mixed, 4, 0), mixed)[0:4]
    stream = st_v[...]
    stream = jnp.where(core == 1, pltpu.roll(stream, 4, 0), stream)[0:4]
    out_ref[...] = stream[:, 0:width] + ROUTE * mixed[:, 0:width] / mixed[:, width : width + 1]

    drain(s1.at[pl.ds(0, nc - 1)], ssem.at[0])
    drain(s2.at[pl.ds(0, nk - 1)], ssem.at[1])
    drain(s4.at[pl.ds(0, nk - 1)], ssem.at[3])
    drain(r5.at[pl.ds(0, nk - 1)], ssem.at[4])
    drain(r6.at[pl.ds(0, ne - 1)], ssem.at[5])

    @pl.when(owner)
    def _():
        drain(r6.at[pl.ds(0, ne - 1)], ssem.at[2])
        pltpu.make_async_copy(st_v, st_v, pair_send.at[4]).wait()

    @pl.when(jnp.logical_not(owner))
    def _():
        drain(s2.at[0], ssem.at[1])
        drain(r6.at[0], ssem.at[5])

    for one in swaps:
        one.wait_send()


def per_device(nc, ne, *args):
    (queries, cache, lengths, w_uv, w_out, residual, gain, router, w_gate, w_up, w_down, ids) = args
    nk, half = nc // 2, ne // 2
    width, ff = w_gate.shape[1], w_gate.shape[2]
    batch = 4 * half
    any_space = pl.BlockSpec(memory_space=pl.ANY)
    vmem = lambda *shape, dtype=F32: pltpu.VMEM(shape, dtype)
    half_type = functools.partial(vmem, dtype=BF16)
    like = lambda x: pltpu.VMEM(x.shape, x.dtype)
    gain = gain.reshape(1, width)
    scratch = [
        like(queries), like(cache), pltpu.SMEM(lengths.shape, I32), like(w_uv), like(w_out), like(residual),
        like(gain), like(router),
        half_type(2, WIDE, ff), half_type(2, WIDE, ff), half_type(2, ff, width), like(ids),
        vmem(2, 16, WIDE), vmem(ne, 8, WIDE), vmem(8, WIDE), vmem(8, WIDE),
        half_type(nc, 16, LATENT // 2 + WIDE), half_type(nc, 16, LATENT // 2 + WIDE),
        vmem(nk, 8, WIDE), vmem(nc, 8, WIDE),
        vmem(half, 8, WIDE),
        half_type(nk, 2 * batch + 16, WIDE), half_type(nk, 2 * batch + 16, WIDE),
        half_type(batch, WIDE), half_type(nk, batch, WIDE),
        vmem(2, half // 2, 8, WIDE), vmem(ne, 8, WIDE),
        pltpu.SemaphoreType.DMA((12,)),
        pltpu.SemaphoreType.DMA((5,)), pltpu.SemaphoreType.DMA((5,)),
        pltpu.SemaphoreType.DMA((6,)), pltpu.SemaphoreType.DMA((6,)),
    ]
    return pl.pallas_call(
        functools.partial(kernel, nc, ne),
        out_shape=jax.ShapeDtypeStruct((4, width), F32),
        in_specs=[any_space] * 12,
        out_specs=pl.BlockSpec(memory_space=pltpu.VMEM),
        scratch_shapes=scratch,
        compiler_params=pltpu.CompilerParams(
            collective_id=0, has_side_effects=True, vmem_limit_bytes=40 * 1024 * 1024
        ),
    )(queries, cache, lengths, w_uv, w_out, residual, gain, router, w_gate, w_up, w_down, ids)


def solution(mesh):
    in_specs = (
        P("ep", None, None),
        P("ep", "ctx", None),
        P("ep"),
        P("ctx", None, None),
        P("ctx", None),
        P("ep", "ctx"),
        P("ctx"),
        P("ep", "ctx"),
        P("ep", "ctx", None),
        P("ep", "ctx", None),
        P("ep", None, "ctx"),
        P("ep", None),
    )
    return jax.shard_map(
        functools.partial(per_device, mesh.shape["ctx"], mesh.shape["ep"]),
        mesh=mesh, in_specs=in_specs, out_specs=P("ep", "ctx"), check_vma=False,
    )
```

time: 438 us -> 72.8 us (0.17)
  waiting for transfers between devices: 199 us -> 0 us
  blocking collectives: 155 us -> 0 us
  Pallas kernels: 0 us -> 60.6 us
  other arithmetic: 40.1 us -> 0 us
  between operations: 13.3 us -> 0.03 us
  starting transfers between devices: 12.1 us -> 0 us
  matrix products: 9.44 us -> 0 us
  local copies, waits for them, and re-layouts: 4.36 us -> 11.7 us
    unnamed x4 -> x0, waiting for transfers between devices: 99.2 us -> none
    psum x1 -> x0, blocking collectives: 65.8 us -> none  [per_device(): lax.psum((gate_part, up_part, squares, logit_part), 'ctx')]
    pallas_call x0 -> x1, Pallas kernels: none -> 60.6 us  [per_device(): pl.pallas_call(functools.partial(kernel, nc, ne), out_shape=jax.ShapeDtyp...]
    all_gather x2 -> x0, blocking collectives: 52.1 us -> none  [merged_2(): everything = jax.tree.map(lambda part: lax.all_gather(part, axis), x)]
    psum x1 -> x0, waiting for transfers between devices: 48.1 us -> none  [per_device(): lax.psum((gate_part, up_part, squares, logit_part), 'ctx')]
    all_gather x1 -> x0, waiting for transfers between devices: 40.8 us -> none  [merged_2(): everything = jax.tree.map(lambda part: lax.all_gather(part, axis), x)]
    add x64 -> x0, other arithmetic: 38.4 us -> none  [the longest x31 37.6 us: combine(): left[..., None] * first[2] + right[..., None] * second[2]]
    all_to_all x2 -> x0, blocking collectives: 37 us -> none  [the longest x1 23.2 us: per_device(): lax.all_to_all(outgoing, 'ep', split_axis=0, concat_axis=0, tiled=True)]
  transfers between devices with their start and end apart: 4 -> 0, of which waited for: 4 -> 0; matrix products, arithmetic and copies ran while one was open for 0% -> 0% of each run, Pallas kernels for 0% -> 0%
where the time goes in v1:
time: 72.8 us; the launch traced here: 72.4 us
  Pallas kernels  60.6 us (83%)
  local copies, waits for them, and re-layouts  11.7 us (16%)
    pallas_call x1, Pallas kernels, per_device(): pl.pallas_call(functools.partial(kernel, nc, ne), out_shape=jax.ShapeDtyp...  60.6 us
    unnamed x24, local copies, waits for them, and re-layouts  11.7 us

profile of v1, /device:TPU:1, one launch (start us, length us, event | category | flops | bytes accessed | tf_op | source)
XLA Modules:
  0.0 72.4 jit_solution(16676768712383681224)
XLA Ops:
  0.0 1.3 %copy.13.wd_h = bf16[1,2048,112]{2,1,0:T(8,128)(2,1)S(1)} copy(bf16[1,2048,112]{1,2,0:T(8,128)(2,1)} %param.22) | data formatting | bytes 917504 | tf_op args[10]
  1.3 0.0 copy-start
  1.3 1.5 %copy-done = bf16[256,3584]{1,0:T(8,128)(2,1)S(1)} copy-done((bf16[256,3584]{1,0:T(8,128)(2,1)S(1)}, bf16[256,3584]{1,0:T(8,128)(2,1)}, u32[]{:S(2)}) %copy-start) | copy-done | bytes 1835032
  2.8 0.0 copy-start.1
  2.8 1.0 %copy-done.1 = bf16[4,96,576]{2,1,0:T(8,128)(2,1)S(1)} copy-done((bf16[4,96,576]{2,1,0:T(8,128)(2,1)S(1)}, bf16[4,96,576]{2,1,0:T(8,128)(2,1)}, u32[]{:S(2)}) %copy-start.1) | copy-done | bytes 442392
  3.8 0.0 copy-start.2
  3.8 1.0 %copy-done.2 = bf16[1,112,2048]{2,1,0:T(8,128)(2,1)S(1)} copy-done((bf16[1,112,2048]{2,1,0:T(8,128)(2,1)S(1)}, bf16[1,112,2048]{2,1,0:T(8,128)(2,1)}, u32[]{:S(2)}) %copy-start.2) | copy-done | bytes 458776
  4.9 0.0 copy-start.3
  4.9 1.0 %copy-done.3 = bf16[1,112,2048]{2,1,0:T(8,128)(2,1)S(1)} copy-done((bf16[1,112,2048]{2,1,0:T(8,128)(2,1)S(1)}, bf16[1,112,2048]{2,1,0:T(8,128)(2,1)}, u32[]{:S(2)}) %copy-start.3) | copy-done | bytes 458776
  5.9 0.0 copy-start.4
  5.9 1.0 %copy-done.4 = bf16[4,64,576]{2,1,0:T(8,128)(2,1)S(1)} copy-done((bf16[4,64,576]{2,1,0:T(8,128)(2,1)S(1)}, bf16[4,64,576]{2,1,0:T(8,128)(2,1)}, u32[]{:S(2)}) %copy-start.4) | copy-done | bytes 294936
  6.8 0.0 copy-start.5
  6.8 0.9 %copy-done.5 = bf16[2,512,128]{2,1,0:T(8,128)(2,1)S(1)} copy-done((bf16[2,512,128]{2,1,0:T(8,128)(2,1)S(1)}, bf16[2,512,128]{2,1,0:T(8,128)(2,1)}, u32[]{:S(2)}) %copy-start.5) | copy-done | bytes 262168
  7.8 0.0 copy-start.6
  7.8 0.7 copy-done.6
  8.5 0.0 copy-start.7
  8.5 0.7 copy-done.7
  9.2 0.0 copy-start.8
  9.2 0.7 copy-done.8
  9.8 0.0 copy-start.9
  9.8 0.7 copy-done.9
  10.5 0.0 copy-start.10
  10.5 0.7 copy-done.10
  11.1 60.6 %shard_map.118 = f32[4,112]{1,0:T(4,128)S(1)} custom-call(bf16[4,64,576]{2,1,0:T(8,128)(2,1)S(1)} %copy-done.4, bf16[4,96,576]{2,1,0:T(8,128)(2,1)S(1)} %copy-done.1, s32[4]{0:T(128)S(1)} %copy-done.8, bf16[2,512,128]{2,1,0:T(8,128)(2,1)S(1)} %copy-done.5, bf16[256,3584]{1,0:T(8,128)(2,1)S(1)} %copy-done, bf16[4,112]{1,0:T(4,128)(2,1)S(1)} %copy-done.7, ...), custom_call_target="tpu_custom_call" | custom-call | tf_op jit(solution)/shard_map/pallas_call | solution.py:385
  71.8 0.6 copy.15
Async XLA Ops:
  1.3 1.5 %copy-start = (bf16[256,3584]{1,0:T(8,128)(2,1)S(1)}, bf16[256,3584]{1,0:T(8,128)(2,1)}, u32[]{:S(2)}) copy-start(bf16[256,3584]{1,0:T(8,128)(2,1)} %wout_h.1) | copy-start | bytes 5505028
  2.8 1.0 %copy-start.1 = (bf16[4,96,576]{2,1,0:T(8,128)(2,1)S(1)}, bf16[4,96,576]{2,1,0:T(8,128)(2,1)}, u32[]{:S(2)}) copy-start(bf16[4,96,576]{2,1,0:T(8,128)(2,1)} %cache_h.1) | copy-start | bytes 1327108
  3.8 1.0 %copy-start.2 = (bf16[1,112,2048]{2,1,0:T(8,128)(2,1)S(1)}, bf16[1,112,2048]{2,1,0:T(8,128)(2,1)}, u32[]{:S(2)}) copy-start(bf16[1,112,2048]{2,1,0:T(8,128)(2,1)} %wg_h.1) | copy-start | bytes 1376260
  4.9 1.0 %copy-start.3 = (bf16[1,112,2048]{2,1,0:T(8,128)(2,1)S(1)}, bf16[1,112,2048]{2,1,0:T(8,128)(2,1)}, u32[]{:S(2)}) copy-start(bf16[1,112,2048]{2,1,0:T(8,128)(2,1)} %wu_h.1) | copy-start | bytes 1376260
  5.9 1.0 %copy-start.4 = (bf16[4,64,576]{2,1,0:T(8,128)(2,1)S(1)}, bf16[4,64,576]{2,1,0:T(8,128)(2,1)}, u32[]{:S(2)}) copy-start(bf16[4,64,576]{2,1,0:T(8,128)(2,1)} %q_h.1) | copy-start | bytes 884740
  6.8 0.9 %copy-start.5 = (bf16[2,512,128]{2,1,0:T(8,128)(2,1)S(1)}, bf16[2,512,128]{2,1,0:T(8,128)(2,1)}, u32[]{:S(2)}) copy-start(bf16[2,512,128]{2,1,0:T(8,128)(2,1)} %wuv_h.1) | copy-start | bytes 786436
  7.8 0.7 copy-start.6
  8.5 0.7 copy-start.7
  9.2 0.7 copy-start.8
  9.8 0.7 copy-start.9
  10.5 0.7 copy-start.10

commit v2 on v1

--- a/solution.py
+++ b/solution.py
@@ -34,7 +34,7 @@
     q_v, cache_v, len_s, wuv_v, wout_v, res_v, gain_v, router_v, wg_v, wu_v, wd_v, ids_v,
     pack, hit_v, st_v, hid_v,
     s1, r1, s2, r2, r3, s4, r4, s5, r5, s6, r6,
-    load_sem, pair_send, pair_recv, ssem, rsem,
+    load_sem, pair_send, pair_recv, ssem, rsem, hello,
 ):
     nk, half = nc // 2, ne // 2
     width = res_h.shape[1]
@@ -62,26 +62,49 @@
         load(8, wout_h, wout_v),
         load(9, wg_h.at[0], wg_v.at[core, pl.ds(0, width)]),
         load(10, wu_h.at[0], wu_v.at[core, pl.ds(0, width)]),
-        load(11, wd_h.at[0], wd_v.at[core]),
+        load(11, wd_h.at[0], wd_v.at[core, pl.ds(0, width)]),
     ]
     for one in loads:
         one.start()
 
+    place = jnp.where((core == 1) & (e >= half), ne - 1 - (e - half), e)
+    base = core * half
+    source = (place >= base) & (place < base + half)
+
+    def at_place(p):
+        return (c, jnp.where((core == 1) & (p >= half), ne - 1 - (p - half), p))
+
     barrier = pltpu.get_barrier_semaphore()
 
+    def greet(to):
+        pl.semaphore_signal(barrier, inc=1, device_id=to, device_id_type=MESH)
+
     def greet_ctx(i, _):
-        pl.semaphore_signal(barrier, inc=1, device_id=(lax.rem(c + i, nc), e), device_id_type=MESH)
+        greet((lax.rem(c + i, nc), e))
         return 0
 
-    def greet_ep(i, _):
-        for f in range(2):
-            pl.semaphore_signal(
-                barrier, inc=1, device_id=(2 * k + f, lax.rem(e + i, ne)), device_id_type=MESH
-            )
+    def greet_ep(p, _):
+        greet(at_place(p))
         return 0
 
     lax.fori_loop(1, nc, greet_ctx, 0)
-    lax.fori_loop(1, ne, greet_ep, 0)
+    first_up = jnp.where(core == 0, jnp.where(source, place + 1, ne), jnp.maximum(place + 1, half))
+    lax.fori_loop(first_up, ne, greet_ep, 0)
+    greeted = jnp.where(core == 0, jnp.minimum(place, half), jnp.where(source, place, 0))
+
+    def answer(p, _):
+        pl.semaphore_signal(hello, inc=1, device_id=at_place(p), device_id_type=MESH)
+        return 0
+
+    xs = 4 if nk % 4 == 0 else nk
+    ys = nk // xs
+    chips = [(dy, dx) for dy in range(ys) for dx in range(xs) if (dy, dx) != (0, 0)]
+    chips.sort(key=lambda o: -min(o[0], ys - o[0]) - min(o[1], xs - o[1]))
+
+    def chip_at(offset):
+        return lax.rem(k // xs + offset[0], ys) * xs + lax.rem(k + offset[1], xs)
+
+    far = sorted(range(1, ne), key=lambda i: -min(i, ne - i))
 
     def remote(src, dst, send, recv, to):
         return pltpu.make_async_remote_copy(
@@ -101,10 +124,11 @@
     blank = jnp.zeros((2, WIDE - width, wg_v.shape[2]), BF16)
     wg_v[:, width:WIDE, :] = blank
     wu_v[:, width:WIDE, :] = blank
-    ids8 = jnp.concatenate([ids_v[...], ids_v[...]], axis=0)
+    wd_v[:, width:WIDE, :] = blank
+    ids = ids_v[...]
     for x in range(ne):
-        hit = jnp.max(jnp.where(ids8 == x, 1.0, 0.0), axis=1, keepdims=True)
-        hit_v[x] = jnp.broadcast_to(hit, (8, WIDE))
+        hit = jnp.max(jnp.where(ids == x, 1.0, 0.0), axis=1, keepdims=True)
+        hit_v[x] = jnp.broadcast_to(hit, (4, WIDE))
 
     loads[0].wait()
     row = iota((rows, rows), 0)
@@ -139,21 +163,23 @@
     s1[:, :, hl:] = jnp.concatenate([peaks, totals], axis=1).astype(BF16)
     r1[pl.ds(c, 1)] = s1[pl.ds(c, 1)]
 
-    pl.semaphore_wait(barrier, nc - 1 + 2 * (ne - 1))
-
-    def send_1(i, _):
-        d = lax.rem(c + i, nc)
+    pl.semaphore_wait(barrier, nc - 1 + greeted)
+    lax.fori_loop(base, jnp.where(source | (core == 0), jnp.minimum(place, base + half), base), answer, 0)
+
+    def send_1(d):
         remote(s1.at[d], r1.at[c], ssem.at[0], rsem.at[0], (d, e)).start()
-        return 0
-
-    lax.fori_loop(1, nc, send_1, 0)
+
+    for offset in chips:
+        for f in range(2):
+            send_1(2 * chip_at(offset) + f)
+    send_1(partner)
 
     mine = pl.ds(0, width)
     swaps = [
         remote(pack.at[core], pack.at[core], pair_send.at[0], pair_recv.at[0], (partner, e)),
         remote(wg_h.at[0], wg_v.at[core, mine], pair_send.at[1], pair_recv.at[1], (partner, e)),
         remote(wu_h.at[0], wu_v.at[core, mine], pair_send.at[2], pair_recv.at[2], (partner, e)),
-        remote(wd_h.at[0], wd_v.at[core], pair_send.at[3], pair_recv.at[3], (partner, e)),
+        remote(wd_h.at[0], wd_v.at[core, mine], pair_send.at[3], pair_recv.at[3], (partner, e)),
     ]
     for one in swaps:
         one.start()
@@ -193,10 +219,11 @@
             a = 2 * width * i
             s2[g + i] = jnp.where(upper, part[:, a : a + WIDE], part[:, a + width : a + width + WIDE])
 
-    def send_2(i, _):
-        d = lax.rem(k + i, nk)
+    def send_2(d):
         remote(s2.at[d], r2.at[c], ssem.at[1], rsem.at[1], (2 * d + side, e)).start()
-        return 0
+
+    for offset in chips:
+        send_2(chip_at(offset))
 
     @pl.when(owner)
     def _():
@@ -204,9 +231,7 @@
 
     @pl.when(jnp.logical_not(owner))
     def _():
-        send_2(0, 0)
-
-    lax.fori_loop(1, nk, send_2, 0)
+        send_2(k)
 
     swaps[0].wait_recv()
 
@@ -220,12 +245,14 @@
         st_v[...] = stream
         r3[pl.ds(lax.rem(e, half), 1)] = hidden[None]
 
-        def send_3(i, _):
+
+        @pl.when(place < ne - 1)
+        def _():
+            pl.semaphore_wait(hello, ne - 1 - place)
+
+        for i in far:
             z = lax.rem(e + i, ne)
             remote(hid_v, r3.at[lax.rem(e, half)], ssem.at[2], rsem.at[2], (c, z)).start()
-            return 0
-
-        lax.fori_loop(1, ne, send_3, 0)
         remote(st_v, st_v, pair_send.at[4], pair_recv.at[4], (partner, e)).start()
         drain(r3.at[pl.ds(0, half - 1)], rsem.at[2])
 
@@ -252,12 +279,12 @@
 
     lane16 = iota((16, WIDE), 1)
     block = jnp.zeros((16, WIDE), F32)
-    place = 0
+    lane_at = 0
     for stat in (squares, logits):
         for piece in split_two(stat):
             for a in range(0, batch, 16):
-                block = jnp.where(lane16 == place, piece[a : a + 16], block)
-                place += 1
+                block = jnp.where(lane16 == lane_at, piece[a : a + 16], block)
+                lane_at += 1
     block = block.astype(BF16)
     for n in (9, 10):
         loads[n].wait()
@@ -270,12 +297,10 @@
         s4[d, 2 * batch :] = block
     r4[pl.ds(k, 1)] = s4[pl.ds(k, 1)]
 
-    def send_4(i, _):
-        d = lax.rem(k + i, nk)
+    for offset in chips:
+        d = chip_at(offset)
         remote(s4.at[d], r4.at[k], ssem.at[3], rsem.at[3], (2 * d + core, e)).start()
-        return 0
-
-    lax.fori_loop(1, nk, send_4, 0)
+
     drain(r4.at[pl.ds(0, nk - 1)], rsem.at[3])
     sums = jnp.sum(r4[...].astype(F32), axis=0)
     gate, up, block = sums[0:batch], sums[batch : 2 * batch], sums[2 * batch :]
@@ -294,36 +319,36 @@
     s5[...] = act
     r5[pl.ds(k, 1)] = act[None]
 
-    def send_5(i, _):
-        d = lax.rem(k + i, nk)
+    for offset in chips:
+        d = chip_at(offset)
         remote(s5, r5.at[k], ssem.at[4], rsem.at[4], (2 * d + core, e)).start()
-        return 0
-
-    lax.fori_loop(1, nk, send_5, 0)
+
     loads[11].wait()
     swaps[3].wait_recv()
     drain(r5.at[pl.ds(0, nk - 1)], rsem.at[4])
     act = jnp.concatenate([r5[d] for d in range(nk)], axis=1)
-    shown = jnp.broadcast_to(score, (batch, WIDE - width))
+    made = lax.dot_general(
+        act, wd_v[...].reshape(2 * WIDE, -1), (((1,), (1,)), ((), ())), preferred_element_type=F32
+    )
+    shown = iota((batch, WIDE), 1) >= width
     for f in range(2):
-        made = jnp.dot(act, wd_v[f], preferred_element_type=F32)
-        made = jnp.concatenate([made, shown], axis=1)
-        s6[f] = made.reshape(half // 2, 8, WIDE)
-
-    def send_6(i, _):
-        t = lax.rem(e + i, half)
-        z = half * core + t
+        s6[f] = jnp.where(shown, score, made[:, f * WIDE : (f + 1) * WIDE]).reshape(half, 4, WIDE)
+
+    def send_6(t, f):
+        remote(s6.at[f, t], r6.at[e], ssem.at[5], rsem.at[5], (2 * k + f, half * core + t)).start()
+
+    turn = lax.rem(e, half)
+    for i in range(half):
+        t = lax.rem(turn + (half // 2 + i), half)
         for f in range(2):
-            @pl.when(jnp.logical_not((f == core) & (z == e)))
-            def _():
-                remote(s6.at[f, t // 2], r6.at[e], ssem.at[5], rsem.at[5], (2 * k + f, z)).start()
-        return 0
-
-    lax.fori_loop(0, half, send_6, 0)
+            if i == half // 2:
+                pl.when(jnp.logical_not(owner & (core == f)))(functools.partial(send_6, t, f))
+            else:
+                send_6(t, f)
 
     @pl.when(owner)
     def _():
-        r6[pl.ds(e, 1)] = s6[core, pl.ds(lax.rem(e, half) // 2, 1)]
+        r6[pl.ds(e, 1)] = s6[core, pl.ds(turn, 1)]
         drain(r6.at[pl.ds(0, ne - 1)], rsem.at[5])
 
     @pl.when(jnp.logical_not(owner))
@@ -332,7 +357,6 @@
         pltpu.make_async_copy(st_v, st_v, pair_recv.at[4]).wait()
 
     mixed = jnp.sum(jnp.where(hit_v[...] > 0.0, r6[...], 0.0), axis=0)
-    mixed = jnp.where(lax.rem(e, 2) == 1, pltpu.roll(mixed, 4, 0), mixed)[0:4]
     stream = st_v[...]
     stream = jnp.where(core == 1, pltpu.roll(stream, 4, 0), stream)[0:4]
     out_ref[...] = stream[:, 0:width] + ROUTE * mixed[:, 0:width] / mixed[:, width : width + 1]
@@ -345,7 +369,8 @@
 
     @pl.when(owner)
     def _():
-        drain(r6.at[pl.ds(0, ne - 1)], ssem.at[2])
+        for _ in far:
+            drain(hid_v, ssem.at[2])
         pltpu.make_async_copy(st_v, st_v, pair_send.at[4]).wait()
 
     @pl.when(jnp.logical_not(owner))
@@ -362,34 +387,35 @@
     nk, half = nc // 2, ne // 2
     width, ff = w_gate.shape[1], w_gate.shape[2]
     batch = 4 * half
-    any_space = pl.BlockSpec(memory_space=pl.ANY)
+    hbm = pl.BlockSpec(memory_space=pltpu.HBM)
     vmem = lambda *shape, dtype=F32: pltpu.VMEM(shape, dtype)
     half_type = functools.partial(vmem, dtype=BF16)
     like = lambda x: pltpu.VMEM(x.shape, x.dtype)
     gain = gain.reshape(1, width)
+    w_down = jnp.swapaxes(w_down, 1, 2)
     scratch = [
         like(queries), like(cache), pltpu.SMEM(lengths.shape, I32), like(w_uv), like(w_out), like(residual),
         like(gain), like(router),
-        half_type(2, WIDE, ff), half_type(2, WIDE, ff), half_type(2, ff, width), like(ids),
-        vmem(2, 16, WIDE), vmem(ne, 8, WIDE), vmem(8, WIDE), vmem(8, WIDE),
+        half_type(2, WIDE, ff), half_type(2, WIDE, ff), half_type(2, WIDE, ff), like(ids),
+        vmem(2, 16, WIDE), vmem(ne, 4, WIDE), vmem(8, WIDE), vmem(8, WIDE),
         half_type(nc, 16, LATENT // 2 + WIDE), half_type(nc, 16, LATENT // 2 + WIDE),
         vmem(nk, 8, WIDE), vmem(nc, 8, WIDE),
         vmem(half, 8, WIDE),
         half_type(nk, 2 * batch + 16, WIDE), half_type(nk, 2 * batch + 16, WIDE),
         half_type(batch, WIDE), half_type(nk, batch, WIDE),
-        vmem(2, half // 2, 8, WIDE), vmem(ne, 8, WIDE),
+        vmem(2, half, 4, WIDE), vmem(ne, 4, WIDE),
         pltpu.SemaphoreType.DMA((12,)),
         pltpu.SemaphoreType.DMA((5,)), pltpu.SemaphoreType.DMA((5,)),
-        pltpu.SemaphoreType.DMA((6,)), pltpu.SemaphoreType.DMA((6,)),
+        pltpu.SemaphoreType.DMA((6,)), pltpu.SemaphoreType.DMA((6,)), pltpu.SemaphoreType.REGULAR,
     ]
     return pl.pallas_call(
         functools.partial(kernel, nc, ne),
         out_shape=jax.ShapeDtypeStruct((4, width), F32),
-        in_specs=[any_space] * 12,
+        in_specs=[hbm] * 12,
         out_specs=pl.BlockSpec(memory_space=pltpu.VMEM),
         scratch_shapes=scratch,
         compiler_params=pltpu.CompilerParams(
-            collective_id=0, has_side_effects=True, vmem_limit_bytes=40 * 1024 * 1024
+            collective_id=0, has_side_effects=True, vmem_limit_bytes=64 * 1024 * 1024
         ),
     )(queries, cache, lengths, w_uv, w_out, residual, gain, router, w_gate, w_up, w_down, ids)
 

time: 72.8 us -> 53.9 us (0.74)
  local copies, waits for them, and re-layouts: 11.7 us -> 1.26 us
  Pallas kernels: 60.6 us -> 52.4 us
    unnamed x24 -> x1, local copies, waits for them, and re-layouts: 11.7 us -> 1.26 us
    pallas_call x1, Pallas kernels: 60.6 us -> 52.4 us  [per_device(): pl.pallas_call(functools.partial(kernel, nc, ne), out_shape=jax.ShapeDtyp...]
where the time goes in v2:
time: 53.9 us; the launch traced here: 53.7 us
  Pallas kernels  52.4 us (97%)
  local copies, waits for them, and re-layouts  1.26 us (2%)
    pallas_call x1, Pallas kernels, per_device(): pl.pallas_call(functools.partial(kernel, nc, ne), out_shape=jax.ShapeDtyp...  52.4 us
    unnamed x1, local copies, waits for them, and re-layouts  1.26 us

profile of v2, /device:TPU:1, one launch (start us, length us, event | category | flops | bytes accessed | tf_op | source)
XLA Modules:
  0.0 53.7 jit_solution(13823087294412381916)
XLA Ops:
  0.0 52.4 %shard_map.118 = f32[4,112]{1,0:T(4,128)} custom-call(bf16[4,64,576]{2,1,0:T(8,128)(2,1)} %q_h.1, bf16[4,96,576]{2,1,0:T(8,128)(2,1)} %cache_h.1, s32[4]{0:T(128)} %len_h.1, bf16[2,512,128]{2,1,0:T(8,128)(2,1)} %wuv_h.1, bf16[256,3584]{1,0:T(8,128)(2,1)} %wout_h.1, bf16[4,112]{1,0:T(4,128)(2,1)} %res_h.1, f32[1,112]{1,0:T(1,128)} %bitcast.3, ...), custom_call_target="tpu_custom_call" | custom-call | tf_op jit(solution)/shard_map/pallas_call | solution.py:411
  52.5 1.3 %copy.14 = f32[4,112]{1,0:T(4,128)} copy(f32[4,112]{1,0:T(4,128)} %shard_map.118) | data formatting | bytes 3584

commit v3 on v2

v3 whole, which is shorter than its diff:
```python
import functools

import jax
import jax.numpy as jnp
from jax import lax
from jax.experimental import pallas as pl
from jax.experimental.pallas import tpu as pltpu
from jax.sharding import PartitionSpec as P

SCALE = 192.0 ** (-0.5)
FLOOR = -1e30
EPS = 1e-06
ROUTE = 2.5
LATENT = 512
WIDE = 128
MESH = pl.DeviceIdType.MESH
BF16, F32, I32 = jnp.bfloat16, jnp.float32, jnp.int32


def iota(shape, dim):
    return lax.broadcasted_iota(I32, shape, dim)


def split_two(x):
    high = x.astype(BF16).astype(F32)
    return high, x - high


def kernel(
    nc,
    ne,
    q_h, cache_h, len_h, wuv_h, wout_h, res_h, gain_h, router_h, wg_h, wu_h, wd_h, ids_h,
    out_ref,
    q_v, cache_v, len_s, wuv_v, wout_v, res_v, gain_v, router_v, wg_v, wu_v, wd_v, ids_v,
    pack, hit_v, st_v, hid_v,
    s1, p1, own_v, own_peak, own_total, m1, r1, s2, r2, r3, s4, r4, s5, r5, score_v, s6, r6,
    load_sem, pair_send, pair_recv, ssem, rsem, hello,
):
    nk, half = nc // 2, ne // 2
    width = res_h.shape[1]
    span = cache_h.shape[1]
    rows = 8 * nc
    split = half // 2
    batch = 4 * split
    c, e = lax.axis_index("ctx"), lax.axis_index("ep")
    k, core = c // 2, lax.rem(c, 2)
    side = e // half
    turn = lax.rem(e, half)
    mine_in = turn // split
    owner = core == side
    partner = 2 * k + 1 - core

    def load(n, src, dst):
        return pltpu.make_async_copy(src, dst, load_sem.at[n])

    loads = [
        load(0, q_h, q_v),
        load(1, cache_h, cache_v),
        load(2, len_h, len_s),
        load(3, res_h, res_v),
        load(4, gain_h, gain_v),
        load(5, router_h, router_v),
        load(6, ids_h, ids_v),
        load(7, wuv_h, wuv_v),
        load(8, wout_h, wout_v),
        load(9, wg_h.at[0], wg_v.at[core, pl.ds(0, width)]),
        load(10, wu_h.at[0], wu_v.at[core, pl.ds(0, width)]),
        load(11, wd_h.at[0], wd_v.at[core, pl.ds(0, width)]),
    ]
    for one in loads:
        one.start()

    place = jnp.where((core == 1) & (e >= half), ne - 1 - (e - half), e)
    base = core * half
    source = (place >= base) & (place < base + half)

    def at_place(p):
        return (c, jnp.where((core == 1) & (p >= half), ne - 1 - (p - half), p))

    xs = 4 if nk % 4 == 0 else nk
    ys = nk // xs
    hops = lambda o: min(o[0], ys - o[0]) + min(o[1], xs - o[1])
    chips = [(dy, dx) for dy in range(ys) for dx in range(xs) if (dy, dx) != (0, 0)]
    chips.sort(key=lambda o: -hops(o))
    remotes = len([o for o in chips if hops(o) > 2])
    here = len(chips)

    def chip_at(offset):
        return lax.rem(k // xs + offset[0], ys) * xs + lax.rem(k + offset[1], xs)

    barrier = pltpu.get_barrier_semaphore()

    def greet(to):
        pl.semaphore_signal(barrier, inc=1, device_id=to, device_id_type=MESH)

    for offset in chips:
        greet((2 * chip_at(offset) + core, e))
    greet((partner, e))

    def greet_ep(p, _):
        greet(at_place(p))
        return 0

    first_up = jnp.where(core == 0, jnp.where(source, place + 1, ne), jnp.maximum(place + 1, half))
    lax.fori_loop(first_up, ne, greet_ep, 0)
    greeted = jnp.where(core == 0, jnp.minimum(place, half), jnp.where(source, place, 0))

    def answer(p, _):
        pl.semaphore_signal(hello, inc=1, device_id=at_place(p), device_id_type=MESH)
        return 0

    far = sorted(range(1, ne), key=lambda i: -min(i, ne - i))

    def remote(src, dst, send, recv, to):
        return pltpu.make_async_remote_copy(
            src_ref=src, dst_ref=dst, send_sem=send, recv_sem=recv, device_id=to, device_id_type=MESH
        )

    def drain(ref, sem):
        pltpu.make_async_copy(ref, ref, sem).wait()

    for one in loads[2:7]:
        one.wait()
    pack[pl.ds(core, 1)] = jnp.zeros((1, 16, WIDE), F32)
    wide_res = res_v[...].astype(F32)
    pack[core, 0:8, 0:width] = jnp.concatenate([wide_res, wide_res], axis=0)
    pack[core, 8:9, 0:width] = gain_v[...]
    pack[core, 9:10, 0:width] = router_v[...].astype(F32)
    blank = jnp.zeros((2, WIDE - width, wg_v.shape[2]), BF16)
    wg_v[:, width:WIDE, :] = blank
    wu_v[:, width:WIDE, :] = blank
    wd_v[:, width:WIDE, :] = blank
    ids = ids_v[...]
    for x in range(ne):
        hit = jnp.max(jnp.where(ids == x, 1.0, 0.0), axis=1, keepdims=True)
        hit_v[x] = jnp.broadcast_to(hit, (4, WIDE))

    loads[0].wait()
    row = iota((rows, rows), 0)
    other = row >= 8 * nk
    want = (row & 3) * (2 * nc) + 4 * ((row >> 3) - jnp.where(other, nk, 0)) + ((row >> 2) & 1)
    want = want + 2 * jnp.where(other, 1 - core, core)
    order = jnp.where(iota((rows, rows), 1) == want, 1.0, 0.0).astype(BF16)
    q = q_v[...].reshape(rows, q_v.shape[2])
    q = jnp.dot(order, q, preferred_element_type=F32).astype(BF16)
    loads[1].wait()
    keys = cache_v[...].reshape(4 * span, cache_v.shape[2])
    scores = lax.dot_general(q, keys, (((1,), (1,)), ((), ())), preferred_element_type=F32) * SCALE
    col = iota((1, 4 * span), 1)
    col_row = jnp.zeros_like(col)
    limit = jnp.full_like(col, len_s[0])
    for r in range(1, 4):
        past = col >= r * span
        col_row = jnp.where(past, r, col_row)
        limit = jnp.where(past, len_s[r], limit)
    position = c * span + col - col_row * span
    col_row = jnp.where(position < limit, col_row, -1)
    valid = (iota((rows, 4 * span), 0) & 3) == col_row
    masked = jnp.where(valid, scores, FLOOR)
    peak = jnp.max(masked, axis=1, keepdims=True).astype(BF16).astype(F32)
    weights = jnp.where(valid, jnp.exp(masked - peak), 0.0).astype(BF16)
    total = jnp.sum(weights.astype(F32), axis=1, keepdims=True)
    summed = jnp.dot(weights, keys[:, :LATENT], preferred_element_type=F32)
    summed = summed.reshape(2, nk, 8, LATENT)
    hl = LATENT // 2
    chunks = range(0, hl, WIDE)
    peaks = jnp.broadcast_to(peak, (rows, WIDE)).reshape(2, nk, 8, WIDE)
    totals = jnp.broadcast_to(total, (rows, WIDE)).reshape(2, nk, 8, WIDE)
    side_lane = iota((nk, 8, WIDE), 2) < 64

    def put(ref, top, amount, parts):
        high, rest = split_two(amount)
        for n, a in enumerate(chunks):
            ref[:, :, a : a + WIDE] = jnp.concatenate([parts[n], parts[n + len(chunks)]], axis=1).astype(BF16)
        ref[:, :, hl:] = jnp.concatenate([top, jnp.where(side_lane, high, rest)], axis=1).astype(BF16)

    columns = range(0, LATENT, WIDE)
    put(s1, peaks[1], totals[1], [summed[1, :, :, a : a + WIDE] for a in columns])
    own_v[...] = summed[0]
    own_peak[...] = peaks[0]
    own_total[...] = totals[0]

    pl.semaphore_wait(barrier, nk + greeted)
    lax.fori_loop(base, jnp.where(source | (core == 0), jnp.minimum(place, base + half), base), answer, 0)

    swap = remote(s1, p1, pair_send.at[5], pair_recv.at[5], (partner, e))
    swap.start()

    mine = pl.ds(0, width)
    swaps = [
        remote(pack.at[core], pack.at[core], pair_send.at[0], pair_recv.at[0], (partner, e)),
        remote(wg_h.at[0], wg_v.at[core, mine], pair_send.at[1], pair_recv.at[1], (partner, e)),
        remote(wu_h.at[0], wu_v.at[core, mine], pair_send.at[2], pair_recv.at[2], (partner, e)),
        remote(wd_h.at[0], wd_v.at[core, mine], pair_send.at[3], pair_recv.at[3], (partner, e)),
    ]
    swap.wait_recv()

    def stats_of(x):
        x = x.astype(F32)
        return x[:, 0:8], x[:, 8:16]

    peaks, totals = stats_of(p1[:, :, hl:])
    totals = totals + pltpu.roll(totals, 64, 2)
    top = jnp.maximum(peaks, own_peak[...])
    from_own, from_other = jnp.exp(own_peak[...] - top), jnp.exp(peaks - top)
    lefts, rights = [], []
    for a in chunks:
        block = p1[:, :, a : a + WIDE].astype(F32)
        lefts.append(from_own * own_v[:, :, a : a + WIDE] + from_other * block[:, 0:8])
        rights.append(from_own * own_v[:, :, hl + a : hl + a + WIDE] + from_other * block[:, 8:16])
    put(m1, top, from_own * own_total[...] + from_other * totals, lefts + rights)
    r1[here] = m1[k]
    for n, offset in enumerate(chips):
        d = chip_at(offset)
        remote(m1.at[d], r1.at[n], ssem.at[0], rsem.at[0], (2 * d + core, e)).start()
    for one in swaps:
        one.start()

    drain(r1.at[pl.ds(0, here)], rsem.at[0])
    peaks, totals = stats_of(r1[:, :, hl:])
    factor = jnp.exp(peaks - jnp.max(peaks, axis=0)[None])
    denom = jnp.sum(factor * totals, axis=0)
    denom = denom[:, 0:1] + denom[:, 64:65]
    columns = []
    for first in (0, 8):
        for a in chunks:
            block = r1[:, :, a : a + WIDE].astype(F32)[:, first : first + 8]
            columns.append(jnp.sum(factor * block, axis=0))
    latent = (jnp.concatenate(columns, axis=1) / denom).astype(BF16)

    loads[7].wait()
    first = jnp.dot(latent, wuv_v[0], preferred_element_type=F32)
    second = jnp.dot(latent, wuv_v[1], preferred_element_type=F32)
    upper = iota((8, WIDE), 0) < 4
    lane = iota((8, WIDE), 1)
    values = jnp.concatenate(
        [
            jnp.where(upper, first, pltpu.roll(first, 4, 0)),
            jnp.where(upper, pltpu.roll(second, 4, 0), second),
        ],
        axis=1,
    ).astype(BF16)
    loads[8].wait()
    group = min(4, nk)
    for g in range(0, nk, group):
        begin, size = 2 * width * g, 2 * width * group
        part = jnp.dot(values, wout_v[:, begin : begin + size], preferred_element_type=F32)
        part = jnp.concatenate([part, jnp.zeros((8, WIDE), F32)], axis=1)
        for i in range(group):
            a = 2 * width * i
            s2[g + i] = jnp.where(upper, part[:, a : a + WIDE], part[:, a + width : a + width + WIDE])

    def send_2(n, d, sem):
        remote(s2.at[d], r2.at[2 * n + core], ssem.at[1], rsem.at[sem], (2 * d + side, e)).start()

    for n, offset in enumerate(chips):
        send_2(n, chip_at(offset), 7 if n < remotes else 1)

    @pl.when(owner)
    def _():
        r2[2 * here + core] = s2[k]

    @pl.when(jnp.logical_not(owner))
    def _():
        send_2(here, k, 1)

    swaps[0].wait_recv()

    @pl.when(owner)
    def _():
        drain(r2.at[pl.ds(0, 2 * (here - remotes) + 1)], rsem.at[1])
        stream = jnp.where(upper, pack[0, 0:8], pack[1, 0:8])
        stream = stream + jnp.sum(r2[2 * remotes :], axis=0)
        if remotes:
            drain(r2.at[pl.ds(0, 2 * remotes)], rsem.at[7])
            stream = stream + jnp.sum(r2[0 : 2 * remotes], axis=0)
        stream = jnp.where(lane < width, stream, 0.0)
        hidden = stream.astype(BF16).astype(F32)
        hid_v[...] = hidden
        st_v[...] = stream
        r3[pl.ds(turn, 1)] = hidden[None]


        @pl.when(place < ne - 1)
        def _():
            pl.semaphore_wait(hello, ne - 1 - place)

        arrived = rsem.at[2 + mine_in]
        for i in far:
            z = lax.rem(e + i, ne)
            remote(hid_v, r3.at[turn], ssem.at[2], arrived, (c, z)).start()
        remote(st_v, st_v, pair_send.at[4], pair_recv.at[4], (partner, e)).start()

    def wait_3(b):
        here_too = owner & (mine_in == b)
        pl.when(here_too)(lambda: drain(r3.at[pl.ds(0, split - 1)], rsem.at[2 + b]))
        pl.when(jnp.logical_not(here_too))(lambda: drain(r3.at[pl.ds(0, split)], rsem.at[2 + b]))

    def send_4(b):
        got = r3[b * split : (b + 1) * split]
        turned = pltpu.roll(got, 4, 1)
        pairs = (split // 2, 2, 8, WIDE)
        top3 = iota((split // 2, 8, WIDE), 1) < 4
        got, turned = got.reshape(pairs), turned.reshape(pairs)
        tokens = [
            jnp.where(top3, got[:, 0], turned[:, 1]).reshape(batch, WIDE),
            jnp.where(top3, turned[:, 0], got[:, 1]).reshape(batch, WIDE),
        ]
        squares = jnp.sum(tokens[0] * tokens[0] + tokens[1] * tokens[1], axis=1, keepdims=True)
        scaled = [(tokens[f] * pack[f, 8:9, :]).astype(BF16) for f in range(2)]
        logits = jnp.sum(
            scaled[0].astype(F32) * pack[0, 9:10, :] + scaled[1].astype(F32) * pack[1, 9:10, :],
            axis=1,
            keepdims=True,
        )
        scaled = jnp.concatenate(scaled, axis=1)
        lane16 = iota((16, WIDE), 1)
        block = jnp.zeros((16, WIDE), F32)
        lane_at = 0
        for stat in (squares, logits):
            for piece in split_two(stat):
                for a in range(0, batch, 16):
                    block = jnp.where(lane16 == lane_at, piece[a : a + 16], block)
                    lane_at += 1
        block = block.astype(BF16)
        gate = jnp.dot(scaled, wg_v[...].reshape(2 * WIDE, -1), preferred_element_type=F32).astype(BF16)
        up = jnp.dot(scaled, wu_v[...].reshape(2 * WIDE, -1), preferred_element_type=F32).astype(BF16)
        for d in range(nk):
            s4[b, d, 0:batch] = gate[:, d * WIDE : (d + 1) * WIDE]
            s4[b, d, batch : 2 * batch] = up[:, d * WIDE : (d + 1) * WIDE]
            s4[b, d, 2 * batch :] = block
        r4[b, here] = s4[b, k]
        for n, offset in enumerate(chips):
            d = chip_at(offset)
            sem = rsem.at[(10 if n < remotes else 8) + b]
            remote(s4.at[b, d], r4.at[b, n], ssem.at[3], sem, (2 * d + core, e)).start()

    def send_5(b):
        drain(r4.at[b, pl.ds(0, here - remotes)], rsem.at[8 + b])
        sums = jnp.sum(r4[b, remotes:].astype(F32), axis=0)
        if remotes:
            drain(r4.at[b, pl.ds(0, remotes)], rsem.at[10 + b])
            sums = sums + jnp.sum(r4[b, 0:remotes].astype(F32), axis=0)
        gate, up, block = sums[0:batch], sums[batch : 2 * batch], sums[2 * batch :]
        parts = batch // 16

        def column(n):
            n = n * parts
            pair = block[:, n : n + parts] + block[:, n + parts : n + 2 * parts]
            return jnp.concatenate([pair[:, a : a + 1] for a in range(parts)], axis=0)

        inverse = lax.rsqrt(column(0) / (width * nc) + EPS)
        score = jax.nn.sigmoid(column(2) * inverse).astype(BF16).astype(F32)
        gate = gate * inverse
        act = gate / (1.0 + jnp.exp(-gate)) * (up * inverse) * score
        act = act.astype(BF16)
        s5[b] = act
        score_v[b] = jnp.broadcast_to(score, (batch, WIDE))
        r5[b, pl.ds(k, 1)] = act[None]
        for offset in chips:
            d = chip_at(offset)
            remote(s5.at[b], r5.at[b, k], ssem.at[4], rsem.at[12 + b], (2 * d + core, e)).start()

    def send_6(b):
        drain(r5.at[b, pl.ds(0, nk - 1)], rsem.at[12 + b])
        act = jnp.concatenate([r5[b, d] for d in range(nk)], axis=1)
        made = lax.dot_general(
            act, wd_v[...].reshape(2 * WIDE, -1), (((1,), (1,)), ((), ())), preferred_element_type=F32
        )
        shown = iota((batch, WIDE), 1) >= width
        for f in range(2):
            block = jnp.where(shown, score_v[b], made[:, f * WIDE : (f + 1) * WIDE])
            s6[f, b * split : (b + 1) * split] = block.reshape(split, 4, WIDE)

        def back(t, f):
            remote(s6.at[f, t], r6.at[e], ssem.at[5], rsem.at[5], (2 * k + f, half * core + t)).start()

        for i in range(1, split + 1):
            t = b * split + lax.rem(turn + i, split)
            for f in range(2):
                if i == split:
                    pl.when(jnp.logical_not(owner & (core == f) & (mine_in == b)))(functools.partial(back, t, f))
                else:
                    back(t, f)

    wait_3(0)
    for n in (9, 10):
        loads[n].wait()
        swaps[n - 8].wait_recv()
    send_4(0)
    wait_3(1)
    send_4(1)
    send_5(0)
    send_5(1)
    loads[11].wait()
    swaps[3].wait_recv()
    send_6(0)
    send_6(1)

    @pl.when(owner)
    def _():
        r6[pl.ds(e, 1)] = s6[core, pl.ds(turn, 1)]
        drain(r6.at[pl.ds(0, ne - 1)], rsem.at[5])

    @pl.when(jnp.logical_not(owner))
    def _():
        drain(r6, rsem.at[5])
        pltpu.make_async_copy(st_v, st_v, pair_recv.at[4]).wait()

    mixed = jnp.sum(jnp.where(hit_v[...] > 0.0, r6[...], 0.0), axis=0)
    stream = st_v[...]
    stream = jnp.where(core == 1, pltpu.roll(stream, 4, 0), stream)[0:4]
    out_ref[...] = stream[:, 0:width] + ROUTE * mixed[:, 0:width] / mixed[:, width : width + 1]

    swap.wait_send()
    drain(s1.at[pl.ds(0, nk - 1)], ssem.at[0])
    drain(s2.at[pl.ds(0, nk - 1)], ssem.at[1])
    for b in range(2):
        drain(s4.at[b, pl.ds(0, nk - 1)], ssem.at[3])
        drain(r5.at[b, pl.ds(0, nk - 1)], ssem.at[4])
    drain(r6.at[pl.ds(0, ne - 1)], ssem.at[5])

    @pl.when(owner)
    def _():
        for _ in far:
            drain(hid_v, ssem.at[2])
        pltpu.make_async_copy(st_v, st_v, pair_send.at[4]).wait()

    @pl.when(jnp.logical_not(owner))
    def _():
        drain(s2.at[0], ssem.at[1])
        drain(r6.at[0], ssem.at[5])

    for one in swaps:
        one.wait_send()


def per_device(nc, ne, *args):
    (queries, cache, lengths, w_uv, w_out, residual, gain, router, w_gate, w_up, w_down, ids) = args
    nk, half = nc // 2, ne // 2
    width, ff = w_gate.shape[1], w_gate.shape[2]
    split = half // 2
    batch = 4 * split
    hbm = pl.BlockSpec(memory_space=pltpu.HBM)
    vmem = lambda *shape, dtype=F32: pltpu.VMEM(shape, dtype)
    half_type = functools.partial(vmem, dtype=BF16)
    like = lambda x: pltpu.VMEM(x.shape, x.dtype)
    gain = gain.reshape(1, width)
    w_down = jnp.swapaxes(w_down, 1, 2)
    scratch = [
        like(queries), like(cache), pltpu.SMEM(lengths.shape, I32), like(w_uv), like(w_out), like(residual),
        like(gain), like(router),
        half_type(2, WIDE, ff), half_type(2, WIDE, ff), half_type(2, WIDE, ff), like(ids),
        vmem(2, 16, WIDE), vmem(ne, 4, WIDE), vmem(8, WIDE), vmem(8, WIDE),
        half_type(nk, 16, LATENT // 2 + WIDE), half_type(nk, 16, LATENT // 2 + WIDE),
        vmem(nk, 8, LATENT), vmem(nk, 8, WIDE), vmem(nk, 8, WIDE),
        half_type(nk, 16, LATENT // 2 + WIDE), half_type(nk, 16, LATENT // 2 + WIDE),
        vmem(nk, 8, WIDE), vmem(nc, 8, WIDE),
        vmem(half, 8, WIDE),
        half_type(2, nk, 2 * batch + 16, WIDE), half_type(2, nk, 2 * batch + 16, WIDE),
        half_type(2, batch, WIDE), half_type(2, nk, batch, WIDE), vmem(2, batch, WIDE),
        vmem(2, half, 4, WIDE), vmem(ne, 4, WIDE),
        pltpu.SemaphoreType.DMA((12,)),
        pltpu.SemaphoreType.DMA((6,)), pltpu.SemaphoreType.DMA((6,)),
        pltpu.SemaphoreType.DMA((6,)), pltpu.SemaphoreType.DMA((14,)), pltpu.SemaphoreType.REGULAR,
    ]
    return pl.pallas_call(
        functools.partial(kernel, nc, ne),
        out_shape=jax.ShapeDtypeStruct((4, width), F32),
        in_specs=[hbm] * 12,
        out_specs=pl.BlockSpec(memory_space=pltpu.VMEM),
        scratch_shapes=scratch,
        compiler_params=pltpu.CompilerParams(
            collective_id=0, has_side_effects=True, vmem_limit_bytes=64 * 1024 * 1024
        ),
    )(queries, cache, lengths, w_uv, w_out, residual, gain, router, w_gate, w_up, w_down, ids)


def solution(mesh):
    in_specs = (
        P("ep", None, None),
        P("ep", "ctx", None),
        P("ep"),
        P("ctx", None, None),
        P("ctx", None),
        P("ep", "ctx"),
        P("ctx"),
        P("ep", "ctx"),
        P("ep", "ctx", None),
        P("ep", "ctx", None),
        P("ep", None, "ctx"),
        P("ep", None),
    )
    return jax.shard_map(
        functools.partial(per_device, mesh.shape["ctx"], mesh.shape["ep"]),
        mesh=mesh, in_specs=in_specs, out_specs=P("ep", "ctx"), check_vma=False,
    )
```

time: 53.9 us -> 48.6 us (0.902)
  Pallas kernels: 52.4 us -> 47.2 us
    pallas_call x1, Pallas kernels: 52.4 us -> 47.2 us  [per_device(): pl.pallas_call(functools.partial(kernel, nc, ne), out_shape=jax.ShapeDtyp...]
where the time goes in v3:
time: 48.6 us; the launch traced here: 48.5 us
  Pallas kernels  47.2 us (97%)
  local copies, waits for them, and re-layouts  1.26 us (3%)
    pallas_call x1, Pallas kernels, per_device(): pl.pallas_call(functools.partial(kernel, nc, ne), out_shape=jax.ShapeDtyp...  47.2 us
    unnamed x1, local copies, waits for them, and re-layouts  1.26 us

profile of v3, /device:TPU:1, one launch (start us, length us, event | category | flops | bytes accessed | tf_op | source)
XLA Modules:
  0.0 48.5 jit_solution(7948693131564028265)
XLA Ops:
  0.0 47.2 %shard_map.118 = f32[4,112]{1,0:T(4,128)} custom-call(bf16[4,64,576]{2,1,0:T(8,128)(2,1)} %q_h.1, bf16[4,96,576]{2,1,0:T(8,128)(2,1)} %cache_h.1, s32[4]{0:T(128)} %len_h.1, bf16[2,512,128]{2,1,0:T(8,128)(2,1)} %wuv_h.1, bf16[256,3584]{1,0:T(8,128)(2,1)} %wout_h.1, bf16[4,112]{1,0:T(4,128)(2,1)} %res_h.1, f32[1,112]{1,0:T(1,128)} %bitcast.3, ...), custom_call_target="tpu_custom_call" | custom-call | tf_op jit(solution)/shard_map/pallas_call | solution.py:467
  47.2 1.3 %copy.14 = f32[4,112]{1,0:T(4,128)} copy(f32[4,112]{1,0:T(4,128)} %shard_map.118) | data formatting | bytes 3584

commit v4 on v3

--- a/solution.py
+++ b/solution.py
@@ -34,7 +34,7 @@
     q_v, cache_v, len_s, wuv_v, wout_v, res_v, gain_v, router_v, wg_v, wu_v, wd_v, ids_v,
     pack, hit_v, st_v, hid_v,
     s1, p1, own_v, own_peak, own_total, m1, r1, s2, r2, r3, s4, r4, s5, r5, score_v, s6, r6,
-    load_sem, pair_send, pair_recv, ssem, rsem, hello,
+    load_sem, pair_send, pair_recv, ssem, rsem, hello, known,
 ):
     nk, half = nc // 2, ne // 2
     width = res_h.shape[1]
@@ -43,9 +43,9 @@
     split = half // 2
     batch = 4 * split
     c, e = lax.axis_index("ctx"), lax.axis_index("ep")
-    k, core = c // 2, lax.rem(c, 2)
+    k, core = c >> 1, c & 1
     side = e // half
-    turn = lax.rem(e, half)
+    turn = e & (half - 1)
     mine_in = turn // split
     owner = core == side
     partner = 2 * k + 1 - core
@@ -67,7 +67,7 @@
         load(10, wu_h.at[0], wu_v.at[core, pl.ds(0, width)]),
         load(11, wd_h.at[0], wd_v.at[core, pl.ds(0, width)]),
     ]
-    for one in loads:
+    for one in loads[:3]:
         one.start()
 
     place = jnp.where((core == 1) & (e >= half), ne - 1 - (e - half), e)
@@ -85,8 +85,10 @@
     remotes = len([o for o in chips if hops(o) > 2])
     here = len(chips)
 
+    peers = {o: ((k // xs + o[0]) & (ys - 1)) * xs + ((k + o[1]) & (xs - 1)) for o in chips}
+
     def chip_at(offset):
-        return lax.rem(k // xs + offset[0], ys) * xs + lax.rem(k + offset[1], xs)
+        return peers[offset]
 
     barrier = pltpu.get_barrier_semaphore()
 
@@ -94,16 +96,24 @@
         pl.semaphore_signal(barrier, inc=1, device_id=to, device_id_type=MESH)
 
     for offset in chips:
-        greet((2 * chip_at(offset) + core, e))
-    greet((partner, e))
+        greet((2 * chip_at(offset) + side, e))
+
+    @pl.when(owner)
+    def _():
+        greet((partner, e))
 
     def greet_ep(p, _):
-        greet(at_place(p))
+        z = at_place(p)[1]
+        greet((2 * k + jnp.where((core == 0) & (place < split), 0, z // half), z))
         return 0
 
     first_up = jnp.where(core == 0, jnp.where(source, place + 1, ne), jnp.maximum(place + 1, half))
     lax.fori_loop(first_up, ne, greet_ep, 0)
-    greeted = jnp.where(core == 0, jnp.minimum(place, half), jnp.where(source, place, 0))
+    greeted = jnp.where(
+        owner,
+        2 * (nk - 1) + place + jnp.where(core == 1, half - split, 0),
+        1 + jnp.where(core == 0, split, 0),
+    )
 
     def answer(p, _):
         pl.semaphore_signal(hello, inc=1, device_id=at_place(p), device_id_type=MESH)
@@ -119,7 +129,119 @@
     def drain(ref, sem):
         pltpu.make_async_copy(ref, ref, sem).wait()
 
-    for one in loads[2:7]:
+    for one in loads[3:7]:
+        one.start()
+
+    def tell_partner():
+        pl.semaphore_signal(known, inc=1, device_id=(partner, e), device_id_type=MESH)
+
+    loads[0].wait()
+    row = iota((rows, rows), 0)
+    other = row >= 8 * nk
+    want = (row & 3) * (2 * nc) + 4 * ((row >> 3) - jnp.where(other, nk, 0)) + ((row >> 2) & 1)
+    want = want + 2 * jnp.where(other, 1 - core, core)
+    order = jnp.where(iota((rows, rows), 1) == want, 1.0, 0.0).astype(BF16)
+    q = q_v[...].reshape(rows, q_v.shape[2])
+    q = jnp.dot(order, q, preferred_element_type=F32).astype(BF16)
+    loads[1].wait()
+    for one in loads[7:]:
+        one.start()
+    loads[2].wait()
+    keys = cache_v[...].reshape(4 * span, cache_v.shape[2])
+    scores = lax.dot_general(q, keys, (((1,), (1,)), ((), ())), preferred_element_type=F32) * SCALE
+    col = iota((1, 4 * span), 1)
+    col_row = jnp.zeros_like(col)
+    limit = jnp.full_like(col, len_s[0])
+    for r in range(1, 4):
+        past = col >= r * span
+        col_row = jnp.where(past, r, col_row)
+        limit = jnp.where(past, len_s[r], limit)
+    position = c * span + col - col_row * span
+    col_row = jnp.where(position < limit, col_row, -1)
+    valid = (iota((rows, 4 * span), 0) & 3) == col_row
+    masked = jnp.where(valid, scores, FLOOR)
+    peak = jnp.max(masked, axis=1, keepdims=True).astype(BF16).astype(F32)
+
+    @pl.when(jnp.logical_not(owner))
+    def _():
+        pl.semaphore_wait(barrier, greeted)
+        tell_partner()
+
+        @pl.when(core == 0)
+        def _():
+            lax.fori_loop(0, split, answer, 0)
+
+    weights = jnp.where(valid, jnp.exp(masked - peak), 0.0).astype(BF16)
+    total = jnp.sum(weights.astype(F32), axis=1, keepdims=True)
+    summed = jnp.dot(weights, keys[:, :LATENT], preferred_element_type=F32)
+    summed = summed.reshape(2, nk, 8, LATENT)
+    hl = LATENT // 2
+    chunks = range(0, hl, WIDE)
+    peaks = jnp.broadcast_to(peak, (rows, WIDE)).reshape(2, nk, 8, WIDE)
+    totals = jnp.broadcast_to(total, (rows, WIDE)).reshape(2, nk, 8, WIDE)
+    side_lane = iota((nk, 8, WIDE), 2) < 64
+
+    def put(ref, top, amount, parts):
+        high, rest = split_two(amount)
+        for n, a in enumerate(chunks):
+            ref[:, :, a : a + WIDE] = jnp.concatenate([parts[n], parts[n + len(chunks)]], axis=1).astype(BF16)
+        ref[:, :, hl:] = jnp.concatenate([top, jnp.where(side_lane, high, rest)], axis=1).astype(BF16)
+
+    columns = range(0, LATENT, WIDE)
+    put(s1, peaks[1], totals[1], [summed[1, :, :, a : a + WIDE] for a in columns])
+    own_v[...] = summed[0]
+    own_peak[...] = peaks[0]
+    own_total[...] = totals[0]
+
+    swap = remote(s1, p1, pair_send.at[5], pair_recv.at[5], (partner, e))
+
+    @pl.when(owner)
+    def _():
+        pl.semaphore_wait(known, 1)
+        swap.start()
+        pl.semaphore_wait(barrier, greeted)
+        tell_partner()
+        lax.fori_loop(base, place, answer, 0)
+
+    pl.when(jnp.logical_not(owner))(swap.start)
+
+    mine = pl.ds(0, width)
+    swaps = [
+        remote(pack.at[core], pack.at[core], pair_send.at[0], pair_recv.at[0], (partner, e)),
+        remote(wg_h.at[0], wg_v.at[core, mine], pair_send.at[1], pair_recv.at[1], (partner, e)),
+        remote(wu_h.at[0], wu_v.at[core, mine], pair_send.at[2], pair_recv.at[2], (partner, e)),
+        remote(wd_h.at[0], wd_v.at[core, mine], pair_send.at[3], pair_recv.at[3], (partner, e)),
+    ]
+    swap.wait_recv()
+
+    def stats_of(x):
+        x = x.astype(F32)
+        return x[:, 0:8], x[:, 8:16]
+
+    peaks, totals = stats_of(p1[:, :, hl:])
+    totals = totals + pltpu.roll(totals, 64, 2)
+    top = jnp.maximum(peaks, own_peak[...])
+    from_own, from_other = jnp.exp(own_peak[...] - top), jnp.exp(peaks - top)
+    lefts, rights = [], []
+    for a in chunks:
+        block = p1[:, :, a : a + WIDE].astype(F32)
+        lefts.append(from_own * own_v[:, :, a : a + WIDE] + from_other * block[:, 0:8])
+        rights.append(from_own * own_v[:, :, hl + a : hl + a + WIDE] + from_other * block[:, 8:16])
+    put(m1, top, from_own * own_total[...] + from_other * totals, lefts + rights)
+    r1[here] = m1[k]
+
+    @pl.when(jnp.logical_not(owner))
+    def _():
+        pl.semaphore_wait(known, 1)
+
+    for n, offset in enumerate(chips):
+        d = chip_at(offset)
+        remote(m1.at[d], r1.at[n], ssem.at[0], rsem.at[0], (2 * d + core, e)).start()
+    @pl.when((core == 0) & jnp.logical_not(owner))
+    def _():
+        lax.fori_loop(split, half, answer, 0)
+
+    for one in loads[3:7]:
         one.wait()
     pack[pl.ds(core, 1)] = jnp.zeros((1, 16, WIDE), F32)
     wide_res = res_v[...].astype(F32)
@@ -135,84 +257,6 @@
         hit = jnp.max(jnp.where(ids == x, 1.0, 0.0), axis=1, keepdims=True)
         hit_v[x] = jnp.broadcast_to(hit, (4, WIDE))
 
-    loads[0].wait()
-    row = iota((rows, rows), 0)
-    other = row >= 8 * nk
-    want = (row & 3) * (2 * nc) + 4 * ((row >> 3) - jnp.where(other, nk, 0)) + ((row >> 2) & 1)
-    want = want + 2 * jnp.where(other, 1 - core, core)
-    order = jnp.where(iota((rows, rows), 1) == want, 1.0, 0.0).astype(BF16)
-    q = q_v[...].reshape(rows, q_v.shape[2])
-    q = jnp.dot(order, q, preferred_element_type=F32).astype(BF16)
-    loads[1].wait()
-    keys = cache_v[...].reshape(4 * span, cache_v.shape[2])
-    scores = lax.dot_general(q, keys, (((1,), (1,)), ((), ())), preferred_element_type=F32) * SCALE
-    col = iota((1, 4 * span), 1)
-    col_row = jnp.zeros_like(col)
-    limit = jnp.full_like(col, len_s[0])
-    for r in range(1, 4):
-        past = col >= r * span
-        col_row = jnp.where(past, r, col_row)
-        limit = jnp.where(past, len_s[r], limit)
-    position = c * span + col - col_row * span
-    col_row = jnp.where(position < limit, col_row, -1)
-    valid = (iota((rows, 4 * span), 0) & 3) == col_row
-    masked = jnp.where(valid, scores, FLOOR)
-    peak = jnp.max(masked, axis=1, keepdims=True).astype(BF16).astype(F32)
-    weights = jnp.where(valid, jnp.exp(masked - peak), 0.0).astype(BF16)
-    total = jnp.sum(weights.astype(F32), axis=1, keepdims=True)
-    summed = jnp.dot(weights, keys[:, :LATENT], preferred_element_type=F32)
-    summed = summed.reshape(2, nk, 8, LATENT)
-    hl = LATENT // 2
-    chunks = range(0, hl, WIDE)
-    peaks = jnp.broadcast_to(peak, (rows, WIDE)).reshape(2, nk, 8, WIDE)
-    totals = jnp.broadcast_to(total, (rows, WIDE)).reshape(2, nk, 8, WIDE)
-    side_lane = iota((nk, 8, WIDE), 2) < 64
-
-    def put(ref, top, amount, parts):
-        high, rest = split_two(amount)
-        for n, a in enumerate(chunks):
-            ref[:, :, a : a + WIDE] = jnp.concatenate([parts[n], parts[n + len(chunks)]], axis=1).astype(BF16)
-        ref[:, :, hl:] = jnp.concatenate([top, jnp.where(side_lane, high, rest)], axis=1).astype(BF16)
-
-    columns = range(0, LATENT, WIDE)
-    put(s1, peaks[1], totals[1], [summed[1, :, :, a : a + WIDE] for a in columns])
-    own_v[...] = summed[0]
-    own_peak[...] = peaks[0]
-    own_total[...] = totals[0]
-
-    pl.semaphore_wait(barrier, nk + greeted)
-    lax.fori_loop(base, jnp.where(source | (core == 0), jnp.minimum(place, base + half), base), answer, 0)
-
-    swap = remote(s1, p1, pair_send.at[5], pair_recv.at[5], (partner, e))
-    swap.start()
-
-    mine = pl.ds(0, width)
-    swaps = [
-        remote(pack.at[core], pack.at[core], pair_send.at[0], pair_recv.at[0], (partner, e)),
-        remote(wg_h.at[0], wg_v.at[core, mine], pair_send.at[1], pair_recv.at[1], (partner, e)),
-        remote(wu_h.at[0], wu_v.at[core, mine], pair_send.at[2], pair_recv.at[2], (partner, e)),
-        remote(wd_h.at[0], wd_v.at[core, mine], pair_send.at[3], pair_recv.at[3], (partner, e)),
-    ]
-    swap.wait_recv()
-
-    def stats_of(x):
-        x = x.astype(F32)
-        return x[:, 0:8], x[:, 8:16]
-
-    peaks, totals = stats_of(p1[:, :, hl:])
-    totals = totals + pltpu.roll(totals, 64, 2)
-    top = jnp.maximum(peaks, own_peak[...])
-    from_own, from_other = jnp.exp(own_peak[...] - top), jnp.exp(peaks - top)
-    lefts, rights = [], []
-    for a in chunks:
-        block = p1[:, :, a : a + WIDE].astype(F32)
-        lefts.append(from_own * own_v[:, :, a : a + WIDE] + from_other * block[:, 0:8])
-        rights.append(from_own * own_v[:, :, hl + a : hl + a + WIDE] + from_other * block[:, 8:16])
-    put(m1, top, from_own * own_total[...] + from_other * totals, lefts + rights)
-    r1[here] = m1[k]
-    for n, offset in enumerate(chips):
-        d = chip_at(offset)
-        remote(m1.at[d], r1.at[n], ssem.at[0], rsem.at[0], (2 * d + core, e)).start()
     for one in swaps:
         one.start()
 
@@ -287,7 +331,7 @@
 
         arrived = rsem.at[2 + mine_in]
         for i in far:
-            z = lax.rem(e + i, ne)
+            z = (e + i) & (ne - 1)
             remote(hid_v, r3.at[turn], ssem.at[2], arrived, (c, z)).start()
         remote(st_v, st_v, pair_send.at[4], pair_recv.at[4], (partner, e)).start()
 
@@ -297,7 +341,7 @@
         pl.when(jnp.logical_not(here_too))(lambda: drain(r3.at[pl.ds(0, split)], rsem.at[2 + b]))
 
     def send_4(b):
-        got = r3[b * split : (b + 1) * split]
+        got = r3[pl.ds(b * split, split)]
         turned = pltpu.roll(got, 4, 1)
         pairs = (split // 2, 2, 8, WIDE)
         top3 = iota((split // 2, 8, WIDE), 1) < 4
@@ -370,32 +414,34 @@
         shown = iota((batch, WIDE), 1) >= width
         for f in range(2):
             block = jnp.where(shown, score_v[b], made[:, f * WIDE : (f + 1) * WIDE])
-            s6[f, b * split : (b + 1) * split] = block.reshape(split, 4, WIDE)
+            s6[f, pl.ds(b * split, split)] = block.reshape(split, 4, WIDE)
 
         def back(t, f):
             remote(s6.at[f, t], r6.at[e], ssem.at[5], rsem.at[5], (2 * k + f, half * core + t)).start()
 
         for i in range(1, split + 1):
-            t = b * split + lax.rem(turn + i, split)
+            t = b * split + ((turn + i) & (split - 1))
             for f in range(2):
                 if i == split:
                     pl.when(jnp.logical_not(owner & (core == f) & (mine_in == b)))(functools.partial(back, t, f))
                 else:
                     back(t, f)
 
-    wait_3(0)
+    first = jnp.where((core == 1) & ((e < split) | (e >= ne - split)), 1, 0)
+    second = 1 - first
+    wait_3(first)
     for n in (9, 10):
         loads[n].wait()
         swaps[n - 8].wait_recv()
-    send_4(0)
-    wait_3(1)
-    send_4(1)
-    send_5(0)
-    send_5(1)
+    send_4(first)
+    wait_3(second)
+    send_4(second)
+    send_5(first)
+    send_5(second)
     loads[11].wait()
     swaps[3].wait_recv()
-    send_6(0)
-    send_6(1)
+    send_6(first)
+    send_6(second)
 
     @pl.when(owner)
     def _():
@@ -462,7 +508,7 @@
         vmem(2, half, 4, WIDE), vmem(ne, 4, WIDE),
         pltpu.SemaphoreType.DMA((12,)),
         pltpu.SemaphoreType.DMA((6,)), pltpu.SemaphoreType.DMA((6,)),
-        pltpu.SemaphoreType.DMA((6,)), pltpu.SemaphoreType.DMA((14,)), pltpu.SemaphoreType.REGULAR,
+        pltpu.SemaphoreType.DMA((6,)), pltpu.SemaphoreType.DMA((14,)), pltpu.SemaphoreType.REGULAR, pltpu.SemaphoreType.REGULAR,
     ]
     return pl.pallas_call(
         functools.partial(kernel, nc, ne),

time: 48.6 us -> 48.2 us (level)
  no operation moved by 1% of the time
where the time goes in v4:
time: 48.2 us; the launch traced here: 48.1 us
  Pallas kernels  46.8 us (97%)
  local copies, waits for them, and re-layouts  1.26 us (3%)
    pallas_call x1, Pallas kernels, per_device(): pl.pallas_call(functools.partial(kernel, nc, ne), out_shape=jax.ShapeDtyp...  46.8 us
    unnamed x1, local copies, waits for them, and re-layouts  1.26 us

profile of v4, /device:TPU:1, one launch (start us, length us, event | category | flops | bytes accessed | tf_op | source)
XLA Modules:
  0.0 48.1 jit_solution(2685264859968862033)
XLA Ops:
  0.0 46.8 %shard_map.118 = f32[4,112]{1,0:T(4,128)} custom-call(bf16[4,64,576]{2,1,0:T(8,128)(2,1)} %q_h.1, bf16[4,96,576]{2,1,0:T(8,128)(2,1)} %cache_h.1, s32[4]{0:T(128)} %len_h.1, bf16[2,512,128]{2,1,0:T(8,128)(2,1)} %wuv_h.1, bf16[256,3584]{1,0:T(8,128)(2,1)} %wout_h.1, bf16[4,112]{1,0:T(4,128)(2,1)} %res_h.1, f32[1,112]{1,0:T(1,128)} %bitcast.3, ...), custom_call_target="tpu_custom_call" | custom-call | tf_op jit(solution)/shard_map/pallas_call | solution.py:513
  46.8 1.3 %copy.14 = f32[4,112]{1,0:T(4,128)} copy(f32[4,112]{1,0:T(4,128)} %shard_map.118) | data formatting | bytes 3584

commit v5 on v4

--- a/solution.py
+++ b/solution.py
@@ -512,12 +512,12 @@
     ]
     return pl.pallas_call(
         functools.partial(kernel, nc, ne),
-        out_shape=jax.ShapeDtypeStruct((4, width), F32),
+        out_shape=pltpu.VMEM((4, width), F32),
         in_specs=[hbm] * 12,
         out_specs=pl.BlockSpec(memory_space=pltpu.VMEM),
         scratch_shapes=scratch,
         compiler_params=pltpu.CompilerParams(
-            collective_id=0, has_side_effects=True, vmem_limit_bytes=64 * 1024 * 1024
+            collective_id=0, has_side_effects=True, vmem_limit_bytes=60 * 1024 * 1024
         ),
     )(queries, cache, lengths, w_uv, w_out, residual, gain, router, w_gate, w_up, w_down, ids)
 

time: 48.2 us -> 46.9 us (0.973)
  local copies, waits for them, and re-layouts: 1.26 us -> 0.58 us
  Pallas kernels: 46.8 us -> 46.2 us
    unnamed x1, local copies, waits for them, and re-layouts: 1.26 us -> 0.58 us
    pallas_call x1, Pallas kernels: 46.8 us -> 46.2 us  [per_device(): pl.pallas_call(functools.partial(kernel, nc, ne), out_shape=pltpu.VMEM((4...]
where the time goes in v5:
time: 46.9 us; the launch traced here: 46.8 us
  Pallas kernels  46.2 us (99%)
  local copies, waits for them, and re-layouts  0.58 us (1%)
    pallas_call x1, Pallas kernels, per_device(): pl.pallas_call(functools.partial(kernel, nc, ne), out_shape=pltpu.VMEM((4...  46.2 us

profile of v5, /device:TPU:1, one launch (start us, length us, event | category | flops | bytes accessed | tf_op | source)
XLA Modules:
  0.0 46.8 jit_solution(9849286227642956771)
XLA Ops:
  0.0 46.2 %shard_map.118 = f32[4,112]{1,0:T(4,128)S(1)} custom-call(bf16[4,64,576]{2,1,0:T(8,128)(2,1)} %q_h.1, bf16[4,96,576]{2,1,0:T(8,128)(2,1)} %cache_h.1, s32[4]{0:T(128)} %len_h.1, bf16[2,512,128]{2,1,0:T(8,128)(2,1)} %wuv_h.1, bf16[256,3584]{1,0:T(8,128)(2,1)} %wout_h.1, bf16[4,112]{1,0:T(4,128)(2,1)} %res_h.1, f32[1,112]{1,0:T(1,128)} %bitcast.3, ...), custom_call_target="tpu_custom_call" | custom-call | tf_op jit(solution)/shard_map/pallas_call | solution.py:513
  46.2 0.6 %copy.14 = f32[4,112]{1,0:T(4,128)} copy(f32[4,112]{1,0:T(4,128)S(1)} %shard_map.118) | data formatting | bytes 3584

commit v6 on v5

--- a/solution.py
+++ b/solution.py
@@ -33,7 +33,7 @@
     out_ref,
     q_v, cache_v, len_s, wuv_v, wout_v, res_v, gain_v, router_v, wg_v, wu_v, wd_v, ids_v,
     pack, hit_v, st_v, hid_v,
-    s1, p1, own_v, own_peak, own_total, m1, r1, s2, r2, r3, s4, r4, s5, r5, score_v, s6, r6,
+    s1, p1, own_v, own_peak, own_total, m1, r1, m7, r8, s2, r2, r3, s4, r4, s7, r7, s5, r5, score_v, s6, r6,
     load_sem, pair_send, pair_recv, ssem, rsem, hello, known,
 ):
     nk, half = nc // 2, ne // 2
@@ -227,16 +227,26 @@
         block = p1[:, :, a : a + WIDE].astype(F32)
         lefts.append(from_own * own_v[:, :, a : a + WIDE] + from_other * block[:, 0:8])
         rights.append(from_own * own_v[:, :, hl + a : hl + a + WIDE] + from_other * block[:, 8:16])
-    put(m1, top, from_own * own_total[...] + from_other * totals, lefts + rights)
+    for n, a in enumerate(chunks):
+        m1[:, :, a : a + WIDE] = jnp.concatenate([lefts[n], rights[n]], axis=1).astype(BF16)
+    eight = iota((nk, 8, WIDE), 1) == iota((nk, 8, WIDE), 2)
+    for n, stat in enumerate((top, from_own * own_total[...] + from_other * totals)):
+        m7[:, n : n + 1] = jnp.sum(jnp.where(eight, stat, 0.0), axis=1, keepdims=True)
     r1[here] = m1[k]
+    r8[here] = m7[k]
 
     @pl.when(jnp.logical_not(owner))
     def _():
         pl.semaphore_wait(known, 1)
 
-    for n, offset in enumerate(chips):
-        d = chip_at(offset)
-        remote(m1.at[d], r1.at[n], ssem.at[0], rsem.at[0], (2 * d + core, e)).start()
+    for group in (chips[:remotes], chips[remotes:]):
+        begin = chips.index(group[0]) if group else 0
+        for n, offset in enumerate(group, begin):
+            d = chip_at(offset)
+            remote(m1.at[d], r1.at[n], ssem.at[0], rsem.at[0], (2 * d + core, e)).start()
+        for n, offset in enumerate(group, begin):
+            d = chip_at(offset)
+            remote(m7.at[d], r8.at[n], ssem.at[7], rsem.at[16], (2 * d + core, e)).start()
     @pl.when((core == 0) & jnp.logical_not(owner))
     def _():
         lax.fori_loop(split, half, answer, 0)
@@ -261,10 +271,13 @@
         one.start()
 
     drain(r1.at[pl.ds(0, here)], rsem.at[0])
-    peaks, totals = stats_of(r1[:, :, hl:])
+    drain(r8.at[pl.ds(0, here)], rsem.at[16])
+    peaks, totals = (
+        jnp.sum(jnp.where(eight, r8[:, n : n + 1], 0.0), axis=2, keepdims=True) for n in range(2)
+    )
     factor = jnp.exp(peaks - jnp.max(peaks, axis=0)[None])
     denom = jnp.sum(factor * totals, axis=0)
-    denom = denom[:, 0:1] + denom[:, 64:65]
+    factor = jnp.broadcast_to(factor, (nk, 8, WIDE))
     columns = []
     for first in (0, 8):
         for a in chunks:
@@ -340,6 +353,8 @@
         pl.when(here_too)(lambda: drain(r3.at[pl.ds(0, split - 1)], rsem.at[2 + b]))
         pl.when(jnp.logical_not(here_too))(lambda: drain(r3.at[pl.ds(0, split)], rsem.at[2 + b]))
 
+    diagonal = iota((batch, WIDE), 0) == iota((batch, WIDE), 1)
+
     def send_4(b):
         got = r3[pl.ds(b * split, split)]
         turned = pltpu.roll(got, 4, 1)
@@ -358,26 +373,23 @@
             keepdims=True,
         )
         scaled = jnp.concatenate(scaled, axis=1)
-        lane16 = iota((16, WIDE), 1)
-        block = jnp.zeros((16, WIDE), F32)
-        lane_at = 0
-        for stat in (squares, logits):
-            for piece in split_two(stat):
-                for a in range(0, batch, 16):
-                    block = jnp.where(lane16 == lane_at, piece[a : a + 16], block)
-                    lane_at += 1
-        block = block.astype(BF16)
+        for n, stat in enumerate((squares, logits)):
+            s7[b, n : n + 1] = jnp.sum(jnp.where(diagonal, stat, 0.0), axis=0, keepdims=True)
+        r7[b, here] = s7[b]
         gate = jnp.dot(scaled, wg_v[...].reshape(2 * WIDE, -1), preferred_element_type=F32).astype(BF16)
         up = jnp.dot(scaled, wu_v[...].reshape(2 * WIDE, -1), preferred_element_type=F32).astype(BF16)
         for d in range(nk):
             s4[b, d, 0:batch] = gate[:, d * WIDE : (d + 1) * WIDE]
             s4[b, d, batch : 2 * batch] = up[:, d * WIDE : (d + 1) * WIDE]
-            s4[b, d, 2 * batch :] = block
         r4[b, here] = s4[b, k]
         for n, offset in enumerate(chips):
             d = chip_at(offset)
             sem = rsem.at[(10 if n < remotes else 8) + b]
             remote(s4.at[b, d], r4.at[b, n], ssem.at[3], sem, (2 * d + core, e)).start()
+            if n + 1 == remotes or n + 1 == here:
+                for m in range(0 if n < remotes else remotes, n + 1):
+                    to = (2 * chip_at(chips[m]) + core, e)
+                    remote(s7.at[b], r7.at[b, m], ssem.at[6], rsem.at[14 + b], to).start()
 
     def send_5(b):
         drain(r4.at[b, pl.ds(0, here - remotes)], rsem.at[8 + b])
@@ -385,16 +397,15 @@
         if remotes:
             drain(r4.at[b, pl.ds(0, remotes)], rsem.at[10 + b])
             sums = sums + jnp.sum(r4[b, 0:remotes].astype(F32), axis=0)
-        gate, up, block = sums[0:batch], sums[batch : 2 * batch], sums[2 * batch :]
-        parts = batch // 16
+        gate, up = sums[0:batch], sums[batch:]
+        drain(r7.at[b, pl.ds(0, here)], rsem.at[14 + b])
+        stats = jnp.sum(r7[b], axis=0)
 
         def column(n):
-            n = n * parts
-            pair = block[:, n : n + parts] + block[:, n + parts : n + 2 * parts]
-            return jnp.concatenate([pair[:, a : a + 1] for a in range(parts)], axis=0)
+            return jnp.sum(jnp.where(diagonal, stats[n : n + 1], 0.0), axis=1, keepdims=True)
 
         inverse = lax.rsqrt(column(0) / (width * nc) + EPS)
-        score = jax.nn.sigmoid(column(2) * inverse).astype(BF16).astype(F32)
+        score = jax.nn.sigmoid(column(1) * inverse).astype(BF16).astype(F32)
         gate = gate * inverse
         act = gate / (1.0 + jnp.exp(-gate)) * (up * inverse) * score
         act = act.astype(BF16)
@@ -459,10 +470,12 @@
     out_ref[...] = stream[:, 0:width] + ROUTE * mixed[:, 0:width] / mixed[:, width : width + 1]
 
     swap.wait_send()
-    drain(s1.at[pl.ds(0, nk - 1)], ssem.at[0])
+    drain(m1.at[pl.ds(0, nk - 1)], ssem.at[0])
+    drain(m7.at[pl.ds(0, nk - 1)], ssem.at[7])
     drain(s2.at[pl.ds(0, nk - 1)], ssem.at[1])
     for b in range(2):
         drain(s4.at[b, pl.ds(0, nk - 1)], ssem.at[3])
+        drain(r7.at[b, pl.ds(0, nk - 1)], ssem.at[6])
         drain(r5.at[b, pl.ds(0, nk - 1)], ssem.at[4])
     drain(r6.at[pl.ds(0, ne - 1)], ssem.at[5])
 
@@ -500,15 +513,17 @@
         vmem(2, 16, WIDE), vmem(ne, 4, WIDE), vmem(8, WIDE), vmem(8, WIDE),
         half_type(nk, 16, LATENT // 2 + WIDE), half_type(nk, 16, LATENT // 2 + WIDE),
         vmem(nk, 8, LATENT), vmem(nk, 8, WIDE), vmem(nk, 8, WIDE),
-        half_type(nk, 16, LATENT // 2 + WIDE), half_type(nk, 16, LATENT // 2 + WIDE),
+        half_type(nk, 16, LATENT // 2), half_type(nk, 16, LATENT // 2),
+        vmem(nk, 2, WIDE), vmem(nk, 2, WIDE),
         vmem(nk, 8, WIDE), vmem(nc, 8, WIDE),
         vmem(half, 8, WIDE),
-        half_type(2, nk, 2 * batch + 16, WIDE), half_type(2, nk, 2 * batch + 16, WIDE),
+        half_type(2, nk, 2 * batch, WIDE), half_type(2, nk, 2 * batch, WIDE),
+        vmem(2, 2, WIDE), vmem(2, nk, 2, WIDE),
         half_type(2, batch, WIDE), half_type(2, nk, batch, WIDE), vmem(2, batch, WIDE),
         vmem(2, half, 4, WIDE), vmem(ne, 4, WIDE),
         pltpu.SemaphoreType.DMA((12,)),
         pltpu.SemaphoreType.DMA((6,)), pltpu.SemaphoreType.DMA((6,)),
-        pltpu.SemaphoreType.DMA((6,)), pltpu.SemaphoreType.DMA((14,)), pltpu.SemaphoreType.REGULAR, pltpu.SemaphoreType.REGULAR,
+        pltpu.SemaphoreType.DMA((8,)), pltpu.SemaphoreType.DMA((17,)), pltpu.SemaphoreType.REGULAR, pltpu.SemaphoreType.REGULAR,
     ]
     return pl.pallas_call(
         functools.partial(kernel, nc, ne),

time: 46.9 us -> 46.7 us (level)
  no operation moved by 1% of the time
where the time goes in v6:
time: 46.7 us; the launch traced here: 46.6 us
  Pallas kernels  46 us (99%)
  local copies, waits for them, and re-layouts  0.58 us (1%)
    pallas_call x1, Pallas kernels, per_device(): pl.pallas_call(functools.partial(kernel, nc, ne), out_shape=pltpu.VMEM((4...  46 us

profile of v6, /device:TPU:1, one launch (start us, length us, event | category | flops | bytes accessed | tf_op | source)
XLA Modules:
  0.0 46.6 jit_solution(12178838176834015250)
XLA Ops:
  0.0 46.0 %shard_map.118 = f32[4,112]{1,0:T(4,128)S(1)} custom-call(bf16[4,64,576]{2,1,0:T(8,128)(2,1)} %q_h.1, bf16[4,96,576]{2,1,0:T(8,128)(2,1)} %cache_h.1, s32[4]{0:T(128)} %len_h.1, bf16[2,512,128]{2,1,0:T(8,128)(2,1)} %wuv_h.1, bf16[256,3584]{1,0:T(8,128)(2,1)} %wout_h.1, bf16[4,112]{1,0:T(4,128)(2,1)} %res_h.1, f32[1,112]{1,0:T(1,128)} %bitcast.3, ...), custom_call_target="tpu_custom_call" | custom-call | tf_op jit(solution)/shard_map/pallas_call | solution.py:528
  46.0 0.6 %copy.14 = f32[4,112]{1,0:T(4,128)} copy(f32[4,112]{1,0:T(4,128)S(1)} %shard_map.118) | data formatting | bytes 3584

commit v7 on v6

--- a/solution.py
+++ b/solution.py
@@ -430,13 +430,10 @@
         def back(t, f):
             remote(s6.at[f, t], r6.at[e], ssem.at[5], rsem.at[5], (2 * k + f, half * core + t)).start()
 
-        for i in range(1, split + 1):
-            t = b * split + ((turn + i) & (split - 1))
-            for f in range(2):
-                if i == split:
-                    pl.when(jnp.logical_not(owner & (core == f) & (mine_in == b)))(functools.partial(back, t, f))
-                else:
-                    back(t, f)
+        for i in range(split):
+            t = b * split + i
+            back(t, partner - 2 * k)
+            pl.when(jnp.logical_not(owner & (t == turn)))(functools.partial(back, t, core))
 
     first = jnp.where((core == 1) & ((e < split) | (e >= ne - split)), 1, 0)
     second = 1 - first

time: 46.7 us -> 46.4 us (level)
  no operation moved by 1% of the time
where the time goes in v7:
time: 46.4 us; the launch traced here: 46.3 us
  Pallas kernels  45.7 us (98%)
  local copies, waits for them, and re-layouts  0.58 us (1%)
    pallas_call x1, Pallas kernels, per_device(): pl.pallas_call(functools.partial(kernel, nc, ne), out_shape=pltpu.VMEM((4...  45.7 us

profile of v7, /device:TPU:1, one launch (start us, length us, event | category | flops | bytes accessed | tf_op | source)
XLA Modules:
  0.0 46.3 jit_solution(13420846170465541989)
XLA Ops:
  0.0 45.7 %shard_map.118 = f32[4,112]{1,0:T(4,128)S(1)} custom-call(bf16[4,64,576]{2,1,0:T(8,128)(2,1)} %q_h.1, bf16[4,96,576]{2,1,0:T(8,128)(2,1)} %cache_h.1, s32[4]{0:T(128)} %len_h.1, bf16[2,512,128]{2,1,0:T(8,128)(2,1)} %wuv_h.1, bf16[256,3584]{1,0:T(8,128)(2,1)} %wout_h.1, bf16[4,112]{1,0:T(4,128)(2,1)} %res_h.1, f32[1,112]{1,0:T(1,128)} %bitcast.3, ...), custom_call_target="tpu_custom_call" | custom-call | tf_op jit(solution)/shard_map/pallas_call | solution.py:525
  45.7 0.6 %copy.14 = f32[4,112]{1,0:T(4,128)} copy(f32[4,112]{1,0:T(4,128)S(1)} %shard_map.118) | data formatting | bytes 3584
